TPU v7x, 32 devices: a whole 2x2x4 slice. The times are simulated.
32 devices in a mesh: az: 4 (over z), rng: 2 (over x), dp: 4 (over y, core).
Axes of the slice: x: 2, y: 2, z: 4, core: 2. Of those that a mesh axis runs over, the one named last changes fastest.
Arguments:
- tokens: bfloat16 [4, 64, 32, 512], P('dp', 'az', 'rng'), may hold values from -6 to 6
- qkv_weight: bfloat16 [512, 1536], replicated, may hold values from -0.25 to 0.25
- out_weight: bfloat16 [512, 512], replicated, may hold values from -0.25 to 0.25
- relative_bias: float32 [8, 17, 17], replicated, may hold values from -4 to 260
- cotangent: bfloat16 [4, 64, 32, 512], P('dp', 'az', 'rng'), may hold values from -6 to 6
Outputs:
- grad_tokens: bfloat16 [4, 64, 32, 512], P('dp', 'az', 'rng')
- grad_qkv_weight: float32 [512, 1536], P(('az', 'rng'))
- grad_out_weight: float32 [512, 512], P(('az', 'rng'))
- grad_bias: float32 [8, 17, 17], replicated
All inputs are finite; a program needn't handle non-finite values.
Results may differ from a plain program's by a relative error of at most 0.012.
Values may be sent and summed in bfloat16 or wider, within the bound.
A program may use at most 128 MiB of HBM per device.

v0:
```python
import math

import jax
import jax.numpy as jnp
from jax import lax
from jax.sharding import PartitionSpec as P


def extended(cells, sides, width, closed):
    for axis, dim in sides:
        count = lax.axis_size(axis)
        ends = count if closed else count - 1
        head = lax.slice_in_dim(cells, 0, width, axis=dim)
        tail = lax.slice_in_dim(cells, cells.shape[dim] - width, cells.shape[dim], axis=dim)
        cells = jnp.concatenate(
            [
                lax.ppermute(tail, axis, [(i, (i + 1) % count) for i in range(ends)]),
                cells,
                lax.ppermute(head, axis, [((i + 1) % count, i) for i in range(ends)]),
            ],
            axis=dim,
        )
    return cells


def starts(*values):
    return tuple((jnp.asarray(value).astype(jnp.int32) for value in values))


def selector(length, radius, present):
    span = 2 * radius + 1
    inner = jnp.arange(length)[:, None, None]
    outer = jnp.arange(length + 2 * radius)[None, :, None]
    offset = jnp.arange(span)[None, None, :]
    return ((outer - inner == offset) & present[None, :, None]).astype(jnp.float32)


def window(table, along, across):
    heads = table.shape[0]
    part_bias = jnp.einsum("hxy,jly->hxjl", table, across, precision=lax.Precision.HIGHEST)
    full_bias = jnp.einsum("ikx,hxjl->hijkl", along, part_bias, precision=lax.Precision.HIGHEST)
    row_total = along.shape[0] * across.shape[0]
    col_total = along.shape[1] * across.shape[1]
    inside = (
        jnp.sum(along, axis=2)[:, None, :, None] * jnp.sum(across, axis=2)[None, :, None, :] > 0.5
    )
    return (full_bias.reshape(heads, row_total, col_total), inside.reshape(row_total, col_total))


def bias_grad(d_score, along, across):
    heads = d_score.shape[0]
    shaped = d_score.reshape(
        heads, along.shape[0], across.shape[0], along.shape[1], across.shape[1]
    )
    folded = jnp.einsum("hijkl,ikx->hxjl", shaped, along, precision=lax.Precision.HIGHEST)
    return jnp.einsum("hxjl,jly->hxy", folded, across, precision=lax.Precision.HIGHEST)


def query_side(queries, d_attended, key_rows, value_rows, bias, inside, scale):
    score = (
        jnp.einsum("qhc,khc->hqk", queries, key_rows, preferred_element_type=jnp.float32) * scale
        + bias
    )
    score = jnp.where(inside[None], score, -jnp.inf)
    top = jnp.max(score, axis=2, keepdims=True)
    log_total = top + jnp.log(jnp.sum(jnp.exp(score - top), axis=2, keepdims=True))
    soft_prob = jnp.exp(score - log_total)
    prob_low = soft_prob.astype(jnp.bfloat16)
    attended = jnp.einsum(
        "hqk,khc->qhc", prob_low, value_rows, preferred_element_type=jnp.float32
    ).astype(jnp.bfloat16)
    delta = jnp.einsum("qhc,qhc->hq", d_attended, attended, preferred_element_type=jnp.float32)
    d_prob = jnp.einsum("qhc,khc->hqk", d_attended, value_rows, preferred_element_type=jnp.float32)
    d_score = soft_prob * (d_prob - delta[:, :, None])
    score_low = d_score.astype(jnp.bfloat16)
    d_query = (
        jnp.einsum("hqk,khc->qhc", score_low, key_rows, preferred_element_type=jnp.float32) * scale
    ).astype(jnp.bfloat16)
    return (attended, log_total[:, :, 0], delta, d_query, d_score, score_low, prob_low)


def shards(tokens, qkv_weight, out_weight, relative_bias, cotangent):
    sweeps, azimuth, radial, width = tokens.shape
    heads = relative_bias.shape[0]
    radius = relative_bias.shape[1] // 2
    head_dim = width // heads
    scale = 1.0 / math.sqrt(head_dim)
    local_count = sweeps * azimuth * radial
    flat_tokens = tokens.reshape(local_count, width)
    flat_cot = cotangent.reshape(local_count, width)
    projected = jnp.dot(flat_tokens, qkv_weight, preferred_element_type=jnp.float32).astype(
        jnp.bfloat16
    )
    projected = projected.reshape(sweeps, azimuth, radial, 3 * width)
    queries = projected[..., :width]
    key_value = projected[..., width:]
    d_attended = lax.dot_general(
        flat_cot, out_weight, (((1,), (1,)), ((), ())), preferred_element_type=jnp.float32
    )
    d_attended = d_attended.astype(jnp.bfloat16).reshape(sweeps, azimuth, radial, width)
    key_ext = extended(key_value, (("az", 1), ("rng", 2)), radius, True)
    tile_side = 8
    tiles_az = azimuth // tile_side
    tiles_rg = radial // tile_side
    tile_count = sweeps * tiles_az * tiles_rg
    group = math.gcd(tile_count, 8)
    turns = tile_count // group
    ext_side = tile_side + 2 * radius
    tile_cells = tile_side * tile_side
    ext_cells = ext_side * ext_side
    first_col = lax.axis_index("rng") * radial
    total_cols = lax.axis_size("rng") * radial
    every_col = jnp.ones((ext_side,), dtype=bool)
    along = selector(tile_side, radius, every_col)
    bias_fixed, inside_fixed = window(relative_bias, along, along)

    def locate(counter):
        sweep_at = counter // (tiles_az * tiles_rg)
        leftover = counter % (tiles_az * tiles_rg)
        return (sweep_at, leftover // tiles_rg * tile_side, leftover % tiles_rg * tile_side)

    def inside_of(col_at):
        column = first_col + col_at - radius + jnp.arange(ext_side)
        present = (column >= 0) & (column < total_cols)
        present_cells = jnp.broadcast_to(present[None, :], (ext_side, ext_side)).reshape(ext_cells)
        return inside_fixed & present_cells[None, :]

    def untile(leaf):
        last = leaf.shape[-1]
        shaped = leaf.reshape(sweeps, tiles_az, tiles_rg, tile_side, tile_side, last)
        return shaped.transpose(0, 1, 3, 2, 4, 5).reshape(sweeps, azimuth, radial, last)

    def query_tile(counter):
        sweep_at, row_at, col_at = locate(counter)
        place = starts(sweep_at, row_at, col_at, 0)
        query_block = lax.dynamic_slice(queries, place, (1, tile_side, tile_side, width)).reshape(
            tile_cells, heads, head_dim
        )
        cot_block = lax.dynamic_slice(d_attended, place, (1, tile_side, tile_side, width)).reshape(
            tile_cells, heads, head_dim
        )
        pair_block = lax.dynamic_slice(key_ext, place, (1, ext_side, ext_side, 2 * width)).reshape(
            ext_cells, 2, heads, head_dim
        )
        inside = inside_of(col_at)
        attended, log_total, delta, d_query, d_score, score_low, prob_low = query_side(
            query_block, cot_block, pair_block[:, 0], pair_block[:, 1], bias_fixed, inside, scale
        )
        d_key = (
            jnp.einsum("hqk,qhc->khc", score_low, query_block, preferred_element_type=jnp.float32)
            * scale
        )
        d_value = jnp.einsum(
            "hqk,qhc->khc", prob_low, cot_block, preferred_element_type=jnp.float32
        )
        term = jnp.stack([d_key, d_value], axis=1).reshape(1, ext_side, ext_side, 2 * width)
        return (
            attended.reshape(tile_cells, width),
            log_total.T,
            delta.T,
            d_query.reshape(tile_cells, width),
            d_score,
            term,
        )

    sums_init = jnp.zeros(
        (sweeps, azimuth + 2 * radius, radial + 2 * radius, 2 * width), jnp.float32
    )

    def query_turn(carry, counter):
        part_sums, score_sum = carry
        lanes = counter * group + jnp.arange(group, dtype=jnp.int32)
        attended, log_total, delta, d_query, d_scores, terms = jax.vmap(query_tile)(lanes)
        score_sum = score_sum + jnp.sum(d_scores, axis=0)
        for member in range(group):
            sweep_at, row_at, col_at = locate(lanes[member])
            place = starts(sweep_at, row_at, col_at, 0)
            current = lax.dynamic_slice(part_sums, place, terms[member].shape)
            part_sums = lax.dynamic_update_slice(part_sums, current + terms[member], place)
        return ((part_sums, score_sum), (attended, log_total, delta, d_query))

    init = (sums_init, jnp.zeros((heads, tile_cells, ext_cells), jnp.float32))
    (part_sums, score_total), outputs = lax.scan(
        query_turn, init, jnp.arange(turns, dtype=jnp.int32)
    )
    bias_local = bias_grad(score_total, along, along)
    attended_all, log_all, delta_all, dquery_all = [
        untile(leaf.reshape((tile_count,) + leaf.shape[2:])) for leaf in outputs
    ]
    edge_terms = jnp.concatenate(
        [part_sums[:, :, :radius], part_sums[:, :, radial + radius :]], axis=2
    )
    arrived = extended(edge_terms.astype(jnp.bfloat16), (("rng", 2),), radius, False).astype(
        edge_terms.dtype
    )
    inner = part_sums[:, :, radius : radius + radial]
    inner = inner.at[:, :, :radius].add(arrived[:, :, :radius])
    inner = inner.at[:, :, radial - radius :].add(arrived[:, :, 3 * radius :])
    cycle_terms = jnp.concatenate([inner[:, :radius], inner[:, azimuth + radius :]], axis=1)
    arrived_cycle = extended(cycle_terms.astype(jnp.bfloat16), (("az", 1),), radius, True).astype(
        cycle_terms.dtype
    )
    owned = inner[:, radius : radius + azimuth]
    owned = owned.at[:, :radius].add(arrived_cycle[:, :radius])
    owned = owned.at[:, azimuth - radius :].add(arrived_cycle[:, 3 * radius :])
    grad_pair = owned.astype(jnp.bfloat16)
    grad_qkv = jnp.concatenate([dquery_all, grad_pair], axis=3)
    grad_flat = grad_qkv.reshape(local_count, 3 * width)
    grad_tokens = lax.dot_general(
        grad_flat, qkv_weight, (((1,), (1,)), ((), ())), preferred_element_type=jnp.float32
    )
    grad_tokens = grad_tokens.astype(jnp.bfloat16).reshape(sweeps, azimuth, radial, width)
    local_qkv = lax.dot_general(
        flat_tokens, grad_flat, (((0,), (0,)), ((), ())), preferred_element_type=jnp.float32
    )
    local_out = lax.dot_general(
        attended_all.reshape(local_count, width),
        flat_cot,
        (((0,), (0,)), ((), ())),
        preferred_element_type=jnp.float32,
    )
    share = width // (lax.axis_size("az") * lax.axis_size("rng"))
    total_qkv, total_out, total_bias = lax.psum(
        (local_qkv, local_out, bias_local), ("az", "rng", "dp")
    )
    first_row = lax.axis_index(("az", "rng")) * share
    rows_qkv = lax.dynamic_slice_in_dim(total_qkv, first_row, share, 0)
    rows_out = lax.dynamic_slice_in_dim(total_out, first_row, share, 0)
    return (grad_tokens, rows_qkv, rows_out, total_bias)


def solution(mesh):
    placed = (P("dp", "az", "rng", None), P(), P(), P(), P("dp", "az", "rng", None))
    return jax.shard_map(
        shards,
        mesh=mesh,
        in_specs=placed,
        out_specs=(P("dp", "az", "rng", None), P(("az", "rng"), None), P(("az", "rng"), None), P()),
        check_vma=False,
    )
```

profile of v0, /device:TPU:0, one launch (start us, length us, event | category | flops | bytes accessed | tf_op | source)
XLA Modules:
  0.0 395.4 jit_solution(18086518368612915313)
XLA Ops:
  27.0 7.9 %while.16 = (s32[]{:T(128)}, bf16[1,16,16,512]{3,2,1,0:T(8,128)(2,1)S(1)}, s32[4,4]{1,0:T(4,128)S(1)}, bf16[4,1,8,8,512]{4,3,2,1,0:T(8,128)(2,1)S(1)}, s32[]{:T(128)}) while((s32[]{:T(128)}, bf16[1,16,16,512]{3,2,1,0:T(8,128)(2,1)S(1)}, s32[4,4]{1,0:T(4,128)S(1)}, bf16[4,1,8,8,512]{4,3,2,1,0:T(8,128)(2,1)S(1)}, s32[]{:T(128)}) %tuple.101), condition=%wide.while_cond.6, body=%wide.while_body.6.sunk | while | flops 2 | bytes 131205 | solution.py:139
  36.4 7.5 %while.15 = (s32[]{:T(128)}, bf16[1,16,16,512]{3,2,1,0:T(8,128)(2,1)S(1)}, s32[4,4]{1,0:T(4,128)S(1)}, bf16[4,1,8,8,512]{4,3,2,1,0:T(8,128)(2,1)S(1)}, s32[]{:T(128)}) while((s32[]{:T(128)}, bf16[1,16,16,512]{3,2,1,0:T(8,128)(2,1)S(1)}, s32[4,4]{1,0:T(4,128)S(1)}, bf16[4,1,8,8,512]{4,3,2,1,0:T(8,128)(2,1)S(1)}, s32[]{:T(128)}) %tuple.102), condition=%wide.while_cond.5, body=%wide.while_body.5.sunk | while | flops 2 | bytes 131205 | solution.py:136
  53.0 4.6 %convolution_bitcast_fusion.1 = f32[8,8,8,24,24]{3,4,1,2,0:T(8,128)} fusion(f32[8,17,8,24,1]{1,3,4,2,0:T(8,128)S(1)} %convolution_bitcast_fusion.4, s32[8,24]{1,0:T(8,128)S(1)} %iota_subtract_fusion), kind=kOutput, calls=%fused_computation.19 | convolution fusion | flops 60165312 | bytes 1284864 | tf_op jit(solution)/shard_map/ikx,hxjl->hijkl/dot_general | solution.py:41
  57.6 6.6 %copy.22 = f32[8,8,8,24,24]{4,3,2,1,0:T(8,128)} copy(f32[8,8,8,24,24]{3,4,1,2,0:T(8,128)} %convolution_bitcast_fusion.1) | data formatting | bytes 2359296 | tf_op jit(solution)/shard_map/ikx,hxjl->hijkl/transpose | solution.py:41
  64.2 4.3 %add.387 = f32[8,64,576]{2,1,0:T(8,128)S(1)} reshape(f32[8,8,8,24,24]{4,3,2,1,0:T(8,128)} %copy.22) | data formatting | bytes 2359296 | tf_op jit(solution)/shard_map/while/body/eval_jaxpr/vmap()/add | solution.py:61
  69.3 6.5 %collective-permute-done.3 = bf16[1,32,8,1024]{3,2,1,0:T(8,128)(2,1)} collective-permute-done((bf16[1,32,8,1024]{3,2,1,0:T(8,128)(2,1)}, bf16[1,32,8,1024]{3,2,1,0:T(8,128)(2,1)}, u32[]{:S(2)}, u32[]{:S(2)}) %collective-permute-start.3) | collective-permute-done | bytes 524320 | tf_op jit(solution)/shard_map/ppermute | solution.py:19
  78.6 19.3 %while.14 = (s32[]{:T(128)}, bf16[1,32,32,1024]{3,2,1,0:T(8,128)(2,1)}, s32[4,4]{1,0:T(4,128)S(1)}, bf16[4,1,24,24,1024]{4,3,2,1,0:T(8,128)(2,1)}, s32[]{:T(128)}) while((s32[]{:T(128)}, bf16[1,32,32,1024]{3,2,1,0:T(8,128)(2,1)}, s32[4,4]{1,0:T(4,128)S(1)}, bf16[4,1,24,24,1024]{4,3,2,1,0:T(8,128)(2,1)}, s32[]{:T(128)}) %tuple.95), condition=%wide.while_cond.4, body=%wide.while_body.4.sunk | while | flops 2 | bytes 2360445 | solution.py:142
  79.2 4.3 %bitcast_dynamic-update-slice_fusion.6 = bf16[4,1,24,24,1024]{4,3,2,1,0:T(8,128)(2,1)} fusion(bf16[4,1,24,24,1024]{4,3,2,1,0:T(8,128)(2,1)} %get-tuple-element.306, s32[]{:T(128)S(6)} %copy.71, bf16[1,32,32,1024]{3,2,1,0:T(8,128)(2,1)} %get-tuple-element.309, s32[]{:T(128)} %bitcast.169, s32[]{:T(128)} %bitcast.170), kind=kLoop, calls=%fused_computation.clone.1 | loop fusion | bytes 2360324 | tf_op jit(solution)/shard_map/while/body/eval_jaxpr/vmap()/gather
  84.1 4.2 %bitcast_dynamic-update-slice_fusion.6 = bf16[4,1,24,24,1024]{4,3,2,1,0:T(8,128)(2,1)} fusion(bf16[4,1,24,24,1024]{4,3,2,1,0:T(8,128)(2,1)} %get-tuple-element.306, s32[]{:T(128)S(6)} %copy.71, bf16[1,32,32,1024]{3,2,1,0:T(8,128)(2,1)} %get-tuple-element.309, s32[]{:T(128)} %bitcast.169, s32[]{:T(128)} %bitcast.170), kind=kLoop, calls=%fused_computation.clone.1 | loop fusion | bytes 2360324 | tf_op jit(solution)/shard_map/while/body/eval_jaxpr/vmap()/gather
  88.9 4.3 %bitcast_dynamic-update-slice_fusion.6 = bf16[4,1,24,24,1024]{4,3,2,1,0:T(8,128)(2,1)} fusion(bf16[4,1,24,24,1024]{4,3,2,1,0:T(8,128)(2,1)} %get-tuple-element.306, s32[]{:T(128)S(6)} %copy.71, bf16[1,32,32,1024]{3,2,1,0:T(8,128)(2,1)} %get-tuple-element.309, s32[]{:T(128)} %bitcast.169, s32[]{:T(128)} %bitcast.170), kind=kLoop, calls=%fused_computation.clone.1 | loop fusion | bytes 2360324 | tf_op jit(solution)/shard_map/while/body/eval_jaxpr/vmap()/gather
  93.8 4.2 %bitcast_dynamic-update-slice_fusion.6 = bf16[4,1,24,24,1024]{4,3,2,1,0:T(8,128)(2,1)} fusion(bf16[4,1,24,24,1024]{4,3,2,1,0:T(8,128)(2,1)} %get-tuple-element.306, s32[]{:T(128)S(6)} %copy.71, bf16[1,32,32,1024]{3,2,1,0:T(8,128)(2,1)} %get-tuple-element.309, s32[]{:T(128)} %bitcast.169, s32[]{:T(128)} %bitcast.170), kind=kLoop, calls=%fused_computation.clone.1 | loop fusion | bytes 2360324 | tf_op jit(solution)/shard_map/while/body/eval_jaxpr/vmap()/gather
  98.0 13.1 %reshape.627 = bf16[4,576,2,8,64]{4,3,2,1,0:T(8,128)(2,1)} reshape(bf16[4,1,24,24,1024]{4,3,2,1,0:T(8,128)(2,1)} %get-tuple-element.92) | data formatting | bytes 9437184 | tf_op jit(solution)/shard_map/while/body/eval_jaxpr/vmap()/reshape | solution.py:142
  111.1 8.1 %fusion.80 = (bf16[4,576,1,8,64]{4,3,2,1,0:T(8,128)(2,1)}, bf16[4,576,1,8,64]{4,3,2,1,0:T(8,128)(2,1)}) fusion(bf16[4,576,2,8,64]{4,3,2,1,0:T(8,128)(2,1)} %reshape.627), kind=kLoop, calls=%fused_computation.139 | loop fusion | bytes 9437184 | tf_op jit(solution)/shard_map/while/body/eval_jaxpr/vmap()/slice | solution.py:147
  119.2 6.2 %copy.51 = bf16[4,576,1,8,64]{1,4,3,0,2:T(8,128)(2,1)} copy(bf16[4,576,1,8,64]{4,3,2,1,0:T(8,128)(2,1)} %get-tuple-element.153) | data formatting | bytes 4718592
  125.4 6.2 %copy.50 = bf16[4,576,1,8,64]{1,4,3,0,2:T(8,128)(2,1)} copy(bf16[4,576,1,8,64]{4,3,2,1,0:T(8,128)(2,1)} %get-tuple-element.154) | data formatting | bytes 4718592
  144.1 4.4 %pad_maximum_fusion = (f32[1,576,2,8,64]{1,4,3,0,2:T(8,128)}, f32[1,576,2,8,64]{1,4,3,0,2:T(8,128)}, f32[1,576,2,8,64]{1,4,3,0,2:T(8,128)}, f32[1,576,2,8,64]{1,4,3,0,2:T(8,128)}) fusion(f32[4,576,1,8,64]{1,4,3,0,2:T(8,128)S(1)} %convolution_bitcast_fusion.2, f32[4,576,1,8,64]{1,4,3,0,2:T(8,128)S(1)} %multiply_bitcast_fusion), kind=kLoop, calls=%fused_computation.23 | loop fusion | flops 2359296 | bytes 18874368 | tf_op jit(solution)/shard_map/while/body/eval_jaxpr/vmap()/stack | solution.py:156
  148.5 5.8 %copy.32 = f32[1,576,2,8,64]{4,3,2,1,0:T(8,128)} copy(f32[1,576,2,8,64]{1,4,3,0,2:T(8,128)} %get-tuple-element.149) | data formatting | bytes 4718592 | tf_op jit(solution)/shard_map/while/body/eval_jaxpr/slice | solution.py:179
  154.3 5.0 %squeeze.52 = f32[1,24,24,1024]{3,2,1,0:T(8,128)} reshape(f32[1,576,2,8,64]{4,3,2,1,0:T(8,128)} %copy.32) | data formatting | bytes 4718592 | tf_op jit(solution)/shard_map/while/body/eval_jaxpr/squeeze | solution.py:179
  159.3 5.8 %copy.29 = f32[1,576,2,8,64]{4,3,2,1,0:T(8,128)} copy(f32[1,576,2,8,64]{1,4,3,0,2:T(8,128)} %get-tuple-element.150) | data formatting | bytes 4718592 | tf_op jit(solution)/shard_map/while/body/eval_jaxpr/slice | solution.py:179
  165.1 5.0 %squeeze.45 = f32[1,24,24,1024]{3,2,1,0:T(8,128)} reshape(f32[1,576,2,8,64]{4,3,2,1,0:T(8,128)} %copy.29) | data formatting | bytes 4718592 | tf_op jit(solution)/shard_map/while/body/eval_jaxpr/squeeze | solution.py:179
  170.1 5.8 %copy.30 = f32[1,576,2,8,64]{4,3,2,1,0:T(8,128)} copy(f32[1,576,2,8,64]{1,4,3,0,2:T(8,128)} %get-tuple-element.151) | data formatting | bytes 4718592 | tf_op jit(solution)/shard_map/while/body/eval_jaxpr/slice | solution.py:179
  175.9 5.0 %squeeze.48 = f32[1,24,24,1024]{3,2,1,0:T(8,128)} reshape(f32[1,576,2,8,64]{4,3,2,1,0:T(8,128)} %copy.30) | data formatting | bytes 4718592 | tf_op jit(solution)/shard_map/while/body/eval_jaxpr/squeeze | solution.py:179
  180.9 5.8 %copy.31 = f32[1,576,2,8,64]{4,3,2,1,0:T(8,128)} copy(f32[1,576,2,8,64]{1,4,3,0,2:T(8,128)} %get-tuple-element.152) | data formatting | bytes 4718592 | tf_op jit(solution)/shard_map/while/body/eval_jaxpr/slice | solution.py:179
  186.7 5.0 %squeeze.50 = f32[1,24,24,1024]{3,2,1,0:T(8,128)} reshape(f32[1,576,2,8,64]{4,3,2,1,0:T(8,128)} %copy.31) | data formatting | bytes 4718592 | tf_op jit(solution)/shard_map/while/body/eval_jaxpr/squeeze | solution.py:179
  200.1 4.2 %collective-permute-start.4 = (bf16[1,32,8,1024]{3,2,1,0:T(8,128)(2,1)}, bf16[1,32,8,1024]{3,2,1,0:T(8,128)(2,1)}, u32[]{:S(2)}, u32[]{:S(2)}) collective-permute-start(bf16[1,32,8,1024]{3,2,1,0:T(8,128)(2,1)} %get-tuple-element.155), channel_id=1, source_target_pairs={{0,4},{1,5},{2,6},{3,7},{8,12},{9,13},{10,14},{11,15},{16,20},{17,... | collective-permute-start | bytes 1572872 | tf_op jit(solution)/shard_map/ppermute | solution.py:17
  210.4 4.3 %fusion.29 = bf16[4,64,8,64]{1,3,2,0:T(8,128)(2,1)} fusion(bf16[4,8,64,576]{3,2,1,0:T(8,128)(2,1)} %copy-done.2, bf16[4,576,1,8,64]{1,4,3,0,2:T(8,128)(2,1)} %copy.50), kind=kOutput, calls=%fused_computation.45 | convolution fusion | flops 151257088 | bytes 4980736 | tf_op jit(solution)/shard_map/while/body/eval_jaxpr/vmap(hqk,khc->qhc)/dot_general | solution.py:77
  226.1 3.8 collective-permute-start.7
  231.4 5.7 %collective-permute-done.6 = bf16[1,8,16,1024]{3,2,1,0:T(8,128)(2,1)S(1)} collective-permute-done((bf16[1,8,16,1024]{3,2,1,0:T(8,128)(2,1)S(1)}, bf16[1,8,16,1024]{3,2,1,0:T(8,128)(2,1)S(1)}, u32[]{:S(2)}, u32[]{:S(2)}) %collective-permute-start.6) | collective-permute-done | bytes 262176 | tf_op jit(solution)/shard_map/ppermute | solution.py:17
  240.8 4.0 %reshape.636 = f32[8,8,8,24,24]{4,3,2,1,0:T(8,128)} reshape(f32[8,64,576]{2,1,0:T(8,128)S(1)} %get-tuple-element.173) | data formatting | bytes 2359296 | tf_op jit(solution)/shard_map/reshape | solution.py:52
  244.8 5.0 %convolution_bitcast_fusion.3 = f32[8,17,8,24]{3,1,2,0:T(8,128)S(1)} fusion(f32[8,8,8,24,24]{4,3,2,1,0:T(8,128)} %reshape.636, s32[8,24]{1,0:T(8,128)S(1)} %iota_subtract_fusion), kind=kOutput, calls=%fused_computation.43 | convolution fusion | flops 60165312 | bytes 1284864 | tf_op jit(solution)/shard_map/hijkl,ikx->hxjl/dot_general | solution.py:55
  250.3 43.2 %psum.23 = f32[8,17,17]{2,1,0:T(8,128)S(1)} all-reduce(f32[8,17,17]{2,1,0:T(8,128)S(1)} %convolution_bitcast_fusion.5), channel_id=1, replica_groups=mesh['az'=4,'rng'=2,'dp'=4] {'az','rng','dp'}, use_global_device_ids=true, to_apply=%region_6.7 | all-reduce | flops 2312 | bytes 18496 | tf_op jit(solution)/shard_map/psum | solution.py:223
  295.5 89.1 %all-reduce.3.cloned.1.call-done = (f32[512,1536]{0,1:T(8,128)}, f32[512,512]{1,0:T(8,128)}) async-done(((f32[512,1536]{0,1:T(8,128)}, f32[512,512]{1,0:T(8,128)}), (f32[512,1536]{0,1:T(8,128)}, f32[512,512]{1,0:T(8,128)})) %all-reduce.3.cloned.1.call-update) | async-done | bytes 4194320 | tf_op jit(solution)/shard_map/psum | solution.py:223
  (157 shorter events, 93.1 us)
Async XLA Ops:
  7.2 1.4 copy-start
  7.2 18.3 %copy-start.14 = (bf16[1,16,16,512]{3,2,1,0:T(8,128)(2,1)S(1)}, bf16[1,16,16,512]{3,2,1,0:T(8,128)(2,1)}, u32[]{:S(2)}) copy-start(bf16[1,16,16,512]{3,2,1,0:T(8,128)(2,1)} %param.17) | copy-start | bytes 786436
  7.2 377.4 %all-reduce.3.cloned.1.call-start = ((), (), s32[]{:S(2)}) async-start(), calls=%async_computation | async-start | bytes 8388608 | tf_op jit(solution)/shard_map/psum | solution.py:223
  11.0 37.7 %collective-permute-start = (bf16[1,8,16,1024]{3,2,1,0:T(8,128)(2,1)}, bf16[1,8,16,1024]{3,2,1,0:T(8,128)(2,1)}, u32[]{:S(2)}, u32[]{:S(2)}) collective-permute-start(bf16[1,8,16,1024]{3,2,1,0:T(8,128)(2,1)} %get-tuple-element.161), channel_id=1, source_target_pairs={{0,8},{8,16},{16,24},{24,0},{1,9},{9,17},{17,25},{25,1},{2,10},{10... | collective-permute-start | bytes 786440 | tf_op jit(solution)/shard_map/ppermute | solution.py:17
  14.0 34.7 %collective-permute-start.1 = (bf16[1,8,16,1024]{3,2,1,0:T(8,128)(2,1)}, bf16[1,8,16,1024]{3,2,1,0:T(8,128)(2,1)}, u32[]{:S(2)}, u32[]{:S(2)}) collective-permute-start(bf16[1,8,16,1024]{3,2,1,0:T(8,128)(2,1)} %get-tuple-element.162), channel_id=1, source_target_pairs={{8,0},{16,8},{24,16},{0,24},{9,1},{17,9},{25,17},{1,25},{10,2},{18... | collective-permute-start | bytes 786440 | tf_op jit(solution)/shard_map/ppermute | solution.py:19
  24.5 24.2 %copy-start.9 = (bf16[1,16,16,1024]{3,2,1,0:T(8,128)(2,1)}, bf16[1,16,16,1024]{3,2,1,0:T(8,128)(2,1)S(1)}, u32[]{:S(2)}) copy-start(bf16[1,16,16,1024]{3,2,1,0:T(8,128)(2,1)S(1)} %slice.310) | copy-start | bytes 1572868
  36.4 11.8 %copy-start.19 = (f32[8,17,17]{2,0,1:T(8,128)S(1)}, f32[8,17,17]{2,0,1:T(8,128)}, u32[]{:S(2)}) copy-start(f32[8,17,17]{2,0,1:T(8,128)} %param.16) | copy-start | bytes 27748
  51.0 18.4 %collective-permute-start.2 = (bf16[1,32,8,1024]{3,2,1,0:T(8,128)(2,1)}, bf16[1,32,8,1024]{3,2,1,0:T(8,128)(2,1)}, u32[]{:S(2)}, u32[]{:S(2)}) collective-permute-start(bf16[1,32,8,1024]{3,2,1,0:T(8,128)(2,1)} %get-tuple-element.159), channel_id=1, source_target_pairs={{0,4},{4,0},{1,5},{5,1},{2,6},{6,2},{3,7},{7,3},{8,12},{12,8},{9,1... | collective-permute-start | bytes 1572872 | tf_op jit(solution)/shard_map/ppermute | solution.py:17
  52.7 23.2 %collective-permute-start.3 = (bf16[1,32,8,1024]{3,2,1,0:T(8,128)(2,1)}, bf16[1,32,8,1024]{3,2,1,0:T(8,128)(2,1)}, u32[]{:S(2)}, u32[]{:S(2)}) collective-permute-start(bf16[1,32,8,1024]{3,2,1,0:T(8,128)(2,1)} %get-tuple-element.160), channel_id=1, source_target_pairs={{4,0},{0,4},{5,1},{1,5},{6,2},{2,6},{7,3},{3,7},{12,8},{8,12},{13,... | collective-permute-start | bytes 1572872 | tf_op jit(solution)/shard_map/ppermute | solution.py:19
  134.8 1.5 copy-start.10
  136.3 1.7 copy-start.3
  136.3 2.0 copy-start.11
  142.5 1.6 copy-start.2
  191.7 1.7 copy-start.5
  193.3 1.7 copy-start.7
  195.0 1.7 copy-start.8
  196.7 1.7 copy-start.6
  199.0 8.3 %copy-start.1 = (f32[1,32,32,1024]{3,2,1,0:T(8,128)}, f32[1,32,32,1024]{3,2,1,0:T(8,128)S(1)}, u32[]{:S(2)}) copy-start(f32[1,32,32,1024]{3,2,1,0:T(8,128)S(1)} %add_dynamic-update-slice_fusion) | copy-start | bytes 12582916
  199.0 8.3 %copy-start.12 = (bf16[4,8,64,64]{3,2,1,0:T(8,128)(2,1)S(1)}, bf16[4,8,64,64]{3,2,1,0:T(8,128)(2,1)}, u32[]{:S(2)}) copy-start(bf16[4,8,64,64]{3,2,1,0:T(8,128)(2,1)} %get-tuple-element.172) | copy-start | bytes 786436
  200.1 19.4 %collective-permute-start.4 = (bf16[1,32,8,1024]{3,2,1,0:T(8,128)(2,1)}, bf16[1,32,8,1024]{3,2,1,0:T(8,128)(2,1)}, u32[]{:S(2)}, u32[]{:S(2)}) collective-permute-start(bf16[1,32,8,1024]{3,2,1,0:T(8,128)(2,1)} %get-tuple-element.155), channel_id=1, source_target_pairs={{0,4},{1,5},{2,6},{3,7},{8,12},{9,13},{10,14},{11,15},{16,20},{17,... | collective-permute-start | bytes 1572872 | tf_op jit(solution)/shard_map/ppermute | solution.py:17
  204.3 15.2 %collective-permute-start.5 = (bf16[1,32,8,1024]{3,2,1,0:T(8,128)(2,1)}, bf16[1,32,8,1024]{3,2,1,0:T(8,128)(2,1)}, u32[]{:S(2)}, u32[]{:S(2)}) collective-permute-start(bf16[1,32,8,1024]{3,2,1,0:T(8,128)(2,1)} %get-tuple-element.156), channel_id=1, source_target_pairs={{4,0},{5,1},{6,2},{7,3},{12,8},{13,9},{14,10},{15,11},{20,16},{21,... | collective-permute-start | bytes 1572872 | tf_op jit(solution)/shard_map/ppermute | solution.py:19
  218.1 20.3 %copy-start.17 = (bf16[1,2,8,2,8,512]{5,4,3,2,1,0:T(8,128)(2,1)}, bf16[1,2,8,2,8,512]{5,4,3,2,1,0:T(8,128)(2,1)S(1)}, u32[]{:S(2)}) copy-start(bf16[1,2,8,2,8,512]{5,4,3,2,1,0:T(8,128)(2,1)S(1)} %copy.26) | copy-start | bytes 786436
  222.0 7.9 %copy-start.13 = (bf16[1,2,8,2,8,512]{5,4,3,2,1,0:T(8,128)(2,1)S(1)}, bf16[1,2,8,2,8,512]{5,4,3,2,1,0:T(8,128)(2,1)}, u32[]{:S(2)}) copy-start(bf16[1,2,8,2,8,512]{5,4,3,2,1,0:T(8,128)(2,1)} %copy.35) | copy-start | bytes 786436
  222.0 7.9 %copy-start.15 = (bf16[1,16,16,512]{3,2,1,0:T(8,128)(2,1)S(1)}, bf16[1,16,16,512]{3,2,1,0:T(8,128)(2,1)}, u32[]{:S(2)}) copy-start(bf16[1,16,16,512]{3,2,1,0:T(8,128)(2,1)} %param.17) | copy-start | bytes 786436
  224.6 6.6 %copy-start.4 = (f32[1,32,16,1024]{3,2,1,0:T(8,128)S(1)}, f32[1,32,16,1024]{3,2,1,0:T(8,128)}, u32[]{:S(2)}) copy-start(f32[1,32,16,1024]{3,2,1,0:T(8,128)} %fusion.34) | copy-start | bytes 6291460
  226.1 11.1 %collective-permute-start.6 = (bf16[1,8,16,1024]{3,2,1,0:T(8,128)(2,1)S(1)}, bf16[1,8,16,1024]{3,2,1,0:T(8,128)(2,1)S(1)}, u32[]{:S(2)}, u32[]{:S(2)}) collective-permute-start(bf16[1,8,16,1024]{3,2,1,0:T(8,128)(2,1)S(1)} %get-tuple-element.157), channel_id=1, source_target_pairs={{0,8},{8,16},{16,24},{24,0},{1,9},{9,17},{17,25},{25,1},{2,10},{10... | collective-permute-start | bytes 786440 | tf_op jit(solution)/shard_map/ppermute | solution.py:17
  226.1 12.0 %collective-permute-start.7 = (bf16[1,8,16,1024]{3,2,1,0:T(8,128)(2,1)S(1)}, bf16[1,8,16,1024]{3,2,1,0:T(8,128)(2,1)S(1)}, u32[]{:S(2)}, u32[]{:S(2)}) collective-permute-start(bf16[1,8,16,1024]{3,2,1,0:T(8,128)(2,1)S(1)} %get-tuple-element.158), channel_id=1, source_target_pairs={{8,0},{16,8},{24,16},{0,24},{9,1},{17,9},{25,17},{1,25},{10,2},{18... | collective-permute-start | bytes 786440 | tf_op jit(solution)/shard_map/ppermute | solution.py:19
  231.4 7.0 %copy-start.16 = (bf16[1,16,16,512]{3,2,1,0:T(8,128)(2,1)S(1)}, bf16[1,16,16,512]{3,2,1,0:T(8,128)(2,1)}, u32[]{:S(2)}) copy-start(bf16[1,16,16,512]{3,2,1,0:T(8,128)(2,1)} %param.13) | copy-start | bytes 786436
  244.8 49.4 %copy-start.18 = (bf16[1,2,8,2,8,512]{5,4,3,2,1,0:T(8,128)(2,1)S(1)}, bf16[1,2,8,2,8,512]{5,4,3,2,1,0:T(8,128)(2,1)}, u32[]{:S(2)}) copy-start(bf16[1,2,8,2,8,512]{5,4,3,2,1,0:T(8,128)(2,1)} %copy-done.17) | copy-start | bytes 786436
Sparse Core Ops, SparseCore 0:
  240.9 143.6 all-reduce.2
where the time goes:
time: 398 us; the launch traced here: 395 us
  local copies, waits for them, and re-layouts  157 us (39%)
  waiting for transfers between devices  102 us (26%)
  blocking collectives  43.2 us (11%)
  matrix products  32.3 us (8%)
  between operations  22.3 us (6%)
  other arithmetic  20.9 us (5%)
  starting transfers between devices  16.7 us (4%)
    psum x1, waiting for transfers between devices, shards(): lax.psum((local_qkv, local_out, bias_local), ('az', 'rng', 'dp'))  89.1 us
    psum x1, blocking collectives, shards(): lax.psum((local_qkv, local_out, bias_local), ('az', 'rng', 'dp'))  43.2 us
    gather x36, local copies, waits for them, and re-layouts  34.5 us
    unnamed x47, local copies, waits for them, and re-layouts  24 us
    slice x4, local copies, waits for them, and re-layouts, query_turn(): terms[member]  23.1 us
    squeeze x4, local copies, waits for them, and re-layouts, query_turn(): terms[member]  20.1 us
    reshape x1, local copies, waits for them, and re-layouts, query_tile(): lax.dynamic_slice(key_ext, place, (1, ext_side, ext_side, 2 * width))  13.1 us
    ppermute x4, starting transfers between devices, extended(): lax.ppermute(tail, axis, [(i, (i + 1) % count) for i in range(ends)])  9.01 us
  transfers between devices with their start and end apart: 9, of which 4 were waited for; matrix products, arithmetic and copies ran while one was open for 17% of the time, Pallas kernels for 0%

commit v1 on v0

v1 whole, which is shorter than its diff:
```python
import functools
import math

import jax
import jax.numpy as jnp
from jax import lax
from jax.experimental import pallas as pl
from jax.experimental.pallas import tpu as pltpu
from jax.sharding import PartitionSpec as P

MESH = pl.DeviceIdType.MESH
F32, BF16 = jnp.float32, jnp.bfloat16
NT = (((1,), (1,)), ((), ()))
HIGH = lax.Precision.HIGHEST


def mm(a, b):
    return jnp.dot(a, b, preferred_element_type=F32)


def mm_nt(a, b):
    return lax.dot_general(a, b, NT, preferred_element_type=F32)


class Copies:
    def __init__(self, send, recv):
        self.send, self.recv, self.count, self.made = send, recv, 0, []

    def put(self, src, dst, device):
        copy = pltpu.make_async_remote_copy(
            src_ref=src,
            dst_ref=dst,
            send_sem=self.send.at[self.count],
            recv_sem=self.recv.at[self.count],
            device_id=device,
            device_id_type=MESH,
        )
        copy.start()
        self.count += 1
        self.made.append(copy)
        return copy

    def drain(self):
        for copy in self.made:
            copy.wait_send()


def greet(devices):
    barrier = pltpu.get_barrier_semaphore()
    for device in devices:
        pl.semaphore_signal(barrier, inc=1, device_id=device, device_id_type=MESH)
    pl.semaphore_wait(barrier, len(devices))


def around(rings, rng_at, side):
    return lax.rem(rng_at + (1 if side else rings - 1), rings)


def halo_kernel(rows, rings, sides, tok, xo, xs, edge, send, recv, local):
    az, ring, dp = lax.axis_index("az"), lax.axis_index("rng"), lax.axis_index("dp")
    up, down = lax.rem(az + rows - 1, rows), lax.rem(az + 1, rows)
    others = [around(rings, ring, side) for side in range(sides)]
    greet(
        [(up, ring, dp), (down, ring, dp)]
        + [(at, other, dp) for other in others for at in (up, az, down)]
    )
    copies = Copies(send, recv)
    copies.put(tok.at[pl.ds(0, 128)], xo.at[pl.ds(384, 128)], (up, ring, dp))
    copies.put(tok.at[pl.ds(128, 128)], xo.at[pl.ds(0, 128)], (down, ring, dp))
    cells = tok[...].astype(F32).reshape(16, 16, 512)
    low = cells[:, :8].reshape(128, 512)
    high = cells[:, 8:].reshape(128, 512)
    for side in range(sides):
        if sides == 1:
            part = jnp.where(ring == 0, high, low)
            land = 0
        else:
            part = high if side else low
            land = 1 - side
        edge[side] = part.astype(BF16)
        src, dst, other = edge.at[side], xs.at[land], others[side]
        copies.put(src.at[pl.ds(0, 64)], dst.at[pl.ds(192, 64)], (up, other, dp))
        copies.put(src.at[pl.ds(64, 64)], dst.at[pl.ds(0, 64)], (down, other, dp))
        copies.put(src, dst.at[pl.ds(64, 128)], (az, other, dp))
    own = pltpu.make_async_copy(tok, xo.at[pl.ds(128, 256)], local)
    own.start()
    own.wait()
    for copy in copies.made:
        copy.wait()


def attend_kernel(
    rings, sides, xo, xs, cot, wqkv, wo, rb,
    own_ref, oh_ref, sh_ref, dq_ref, att_ref, gb_ref,
    kv, qs, da, tab, tables, bias, db,
):
    ring = lax.axis_index("rng")
    width = 16 + 8 * sides
    lane = lax.broadcasted_iota(jnp.int32, (1, 128), 1)
    group = lane // 16
    inner = lane - group * 16

    tab[...] = jnp.zeros_like(tab)
    for h in range(8):
        tab[h * 24 : h * 24 + 17, 0:17] = rb[h]

    def column(c):
        if c < 16:
            place = jnp.int32(c)
        elif sides == 1:
            place = jnp.where(ring == 0, c, c - 24)
        else:
            place = jnp.int32(c - 24 if c < 24 else c - 8)
        level = ring * 16 + place
        offset = place - inner + 8
        present = (level >= 0) & (level < rings * 16)
        valid = (offset >= 0) & (offset <= 16) & present
        offset = jnp.where(valid, offset, -1)
        hot = lax.broadcasted_iota(jnp.int32, (128, 128), 0) == offset
        return hot.astype(F32), valid

    for c in range(width):
        hot, valid = column(c)
        filled = jnp.dot(tab[...], hot, precision=HIGH, preferred_element_type=F32)
        tables[pl.ds(c, 192, width), :] = jnp.where(valid, filled, -jnp.inf)

    def pieces(a):
        found = [(a * 16, 16, 0)]
        for s in range(sides):
            found.append((384 + 192 * s + a * 8, 8, 16 + 8 * s))
        return found

    def build(p, carry):
        for hh in range(2):
            base = (2 * p + hh) * 24
            for a in range(24):
                block = jnp.full((width, 128), -jnp.inf, F32)
                for q in range(8):
                    i = a - q
                    if 0 <= i <= 16:
                        at = pl.multiple_of((base + i) * width, 8)
                        block = jnp.where(group == q, tables[pl.ds(at, width), :], block)
                for start, size, first in pieces(a):
                    bias[p, start : start + size, hh * 128 : hh * 128 + 128] = block[
                        first : first + size
                    ]
        return carry

    lax.fori_loop(0, 4, build, 0)

    def project(r, carry):
        at = pl.multiple_of(r * 128, 128)
        kv[pl.ds(at, 128), :] = mm(xo[pl.ds(at, 128), :], wqkv[:, 512:]).astype(BF16)
        return carry

    lax.fori_loop(0, 4, project, 0)
    for s in range(sides):

        def project_side(r, carry):
            at = pl.multiple_of(r * 128, 128)
            kv[pl.ds(512 + 256 * s + at, 128), :] = mm(
                xs[s, pl.ds(at, 128), :], wqkv[:, 512:]
            ).astype(BF16)
            return carry

        lax.fori_loop(0, 2, project_side, 0)
    qs[...] = (mm(xo[128:384, :], wqkv[:, :512]).astype(BF16).astype(F32) * 0.125).astype(BF16)
    da[...] = mm_nt(cot[...], wo[...]).astype(BF16)

    first_half = lax.broadcasted_iota(jnp.int32, (128, 128), 1) < 64

    def diagonal(block):
        wide = block.astype(F32)
        return jnp.concatenate(
            [jnp.where(first_half, wide, 0.0), jnp.where(first_half, 0.0, wide)], axis=0
        ).astype(BF16)

    def fold(block):
        return jnp.concatenate([block[:64, :128], block[64:, 128:]], axis=0)

    def gather(t, cols):
        parts = [kv[t * 128 : t * 128 + 384, cols]]
        for s in range(sides):
            parts.append(kv[512 + 256 * s + 64 * t : 704 + 256 * s + 64 * t, cols])
        return jnp.concatenate(parts, axis=0)

    def pair(p, carry):
        lanes = pl.ds(pl.multiple_of(p * 128, 128), 128)
        v_lanes = pl.ds(pl.multiple_of(512 + p * 128, 128), 128)
        grads = []
        for t in range(2):
            rows = slice(t * 128, t * 128 + 128)
            keys, values = gather(t, lanes), gather(t, v_lanes)
            query, d_out = diagonal(qs[rows, lanes]), diagonal(da[rows, lanes])
            score = mm_nt(keys, query) + bias[p]
            e = jnp.exp(score - jnp.max(score, axis=0, keepdims=True))
            prob = e * (1.0 / jnp.sum(e, axis=0, keepdims=True))
            prob_low = prob.astype(BF16)
            attended = fold(mm(values.T, prob_low)).astype(BF16)
            att_ref[lanes, rows] = attended
            terms = da[rows, lanes].astype(F32).T * attended.astype(F32)
            delta = jnp.concatenate(
                [
                    jnp.sum(terms[:64], axis=0, keepdims=True),
                    jnp.sum(terms[64:], axis=0, keepdims=True),
                ],
                axis=1,
            )
            d_score = prob * (mm_nt(values, d_out) - delta)
            if t == 0:
                db[p] = d_score
            else:
                db[p] = db[p] + d_score
            low = d_score.astype(BF16)
            d_query = fold(mm(keys.T, low)) * 0.125
            dq_ref[rows, lanes] = d_query.T.astype(BF16)
            grads.append((mm(low, query), mm(prob_low, d_out)))
        for kind, cols in ((0, lanes), (1, v_lanes)):
            g0, g1 = grads[0][kind], grads[1][kind]
            own_ref[:, cols] = g0[128:384] + g1[:256]
            oh_ref[0, :, cols] = g0[:128].astype(BF16)
            oh_ref[1, :, cols] = g1[256:384].astype(BF16)
            for s in range(sides):
                b = 384 + 192 * s
                sh_ref[s, 0:64, cols] = g0[b : b + 64].astype(BF16)
                sh_ref[s, 64:192, cols] = (g0[b + 64 : b + 192] + g1[b : b + 128]).astype(BF16)
                sh_ref[s, 192:256, cols] = g1[b + 128 : b + 192].astype(BF16)
        return carry

    lax.fori_loop(0, 4, pair, 0)

    def unbuild(p, carry):
        for hh in range(2):
            base = (2 * p + hh) * 24
            for i in range(17):
                block = jnp.zeros((width, 128), F32)
                for q in range(8):
                    found = [
                        db[p, start : start + size, hh * 128 : hh * 128 + 128]
                        for start, size, _ in pieces(i + q)
                    ]
                    block = jnp.where(group == q, jnp.concatenate(found, axis=0), block)
                tables[pl.ds(pl.multiple_of((base + i) * width, 8), width), :] = block
        return carry

    lax.fori_loop(0, 4, unbuild, 0)
    total = jnp.zeros((192, 128), F32)
    for c in range(width):
        hot, _ = column(c)
        total = total + lax.dot_general(
            tables[pl.ds(c, 192, width), :], hot, NT, precision=HIGH, preferred_element_type=F32
        )
    for h in range(8):
        gb_ref[h] = total[h * 24 : h * 24 + 17, 0:17]


def reduce_kernel(
    rows, rings, sides, share,
    own, oh, sh, dq, att, tok, cot, wqkv,
    gtok, gq, go,
    r_o, r_s, part, r1, ka, kb, rxa, ryb, a2, b2, rya, rxb, z3, rz, gath, send, recv,
):
    az, ring, dp = lax.axis_index("az"), lax.axis_index("rng"), lax.axis_index("dp")
    up, down = lax.rem(az + rows - 1, rows), lax.rem(az + 1, rows)
    others = [around(rings, ring, side) for side in range(sides)]
    y, core = dp // 2, lax.rem(dp, 2)
    mate, over = y * 2 + 1 - core, (1 - y) * 2 + core
    rng_to = [lax.rem(ring + o, rings) for o in range(1, rings)]
    az_to = [lax.rem(az + o, rows) for o in range(1, rows)]
    dp_to = [lax.rem(dp + o, 4) for o in range(1, 4)]
    greet(
        [(az, other, dp) for other in rng_to]
        + [(at, ring, dp) for at in az_to]
        + [(az, ring, other) for other in dp_to]
        + [(at, other, dp) for other in others for at in (up, down)]
    )
    copies = Copies(send, recv)
    back = [
        copies.put(oh.at[0], r_o.at[1], (up, ring, dp)),
        copies.put(oh.at[1], r_o.at[0], (down, ring, dp)),
    ]
    for s in range(sides):
        land = 0 if sides == 1 else 1 - s
        src, dst, other = sh.at[s], r_s.at[land], others[s]
        back.append(copies.put(src.at[pl.ds(0, 64)], dst.at[pl.ds(192, 64)], (up, other, dp)))
        back.append(copies.put(src.at[pl.ds(192, 64)], dst.at[pl.ds(0, 64)], (down, other, dp)))
        back.append(
            copies.put(src.at[pl.ds(64, 128)], dst.at[pl.ds(64, 128)], (az, other, dp))
        )
    box = (rows, rings, share, 512)
    tok_t = tok[...].T

    def pair_up(f):
        return copies.put(part.at[f, 1 - core], r1.at[f], (az, ring, mate))

    def spread(f, first):
        first.wait_recv()
        kept = part[f, core].astype(F32) + r1[f].astype(F32)
        ka[f] = kept[..., :256].astype(BF16)
        kb[f, 0] = kept[..., 256:384].astype(BF16)
        kb[f, 1] = kept[..., 384:].astype(BF16)
        over_x = [
            copies.put(ka.at[f, :, to], rxa.at[f, o], (az, to, dp)) for o, to in enumerate(rng_to)
        ]
        return over_x, copies.put(kb.at[f, 1 - y], ryb.at[f], (az, ring, over))

    def cross(f, state):
        over_x, over_y = state
        for copy in over_x:
            copy.wait_recv()
        kept = ka[f, :, ring].astype(F32)
        for o in range(rings - 1):
            kept = kept + rxa[f, o].astype(F32)
        a2[f, 0] = kept[..., :128].astype(BF16)
        a2[f, 1] = kept[..., 128:].astype(BF16)
        next_y = copies.put(a2.at[f, 1 - y], rya.at[f], (az, ring, over))
        over_y.wait_recv()
        b2[f] = (kb[f, y].astype(F32) + ryb[f].astype(F32)).astype(BF16)
        next_x = [
            copies.put(b2.at[f, :, to], rxb.at[f, o], (az, to, dp)) for o, to in enumerate(rng_to)
        ]
        return next_x, next_y

    def along(f, state):
        over_x, over_y = state
        over_y.wait_recv()
        z3[f, :, 0] = (a2[f, y].astype(F32) + rya[f].astype(F32)).astype(BF16)
        for copy in over_x:
            copy.wait_recv()
        kept = b2[f, :, ring].astype(F32)
        for o in range(rings - 1):
            kept = kept + rxb[f, o].astype(F32)
        z3[f, :, 1] = kept.astype(BF16)
        return [
            copies.put(z3.at[f, to], rz.at[f, o], (to, ring, dp)) for o, to in enumerate(az_to)
        ]

    def collect(f, state):
        for copy in state:
            copy.wait_recv()
        kept = z3[f, az].astype(F32)
        for o in range(rows - 1):
            kept = kept + rz[f, o].astype(F32)
        gath[f, dp] = kept.astype(BF16)
        return [
            copies.put(gath.at[f, dp], gath.at[f, dp], (az, ring, to)) for to in dp_to
        ]

    def finish(f, state):
        for copy in state:
            copy.wait_recv()
        for d in range(4):
            for sub in range(2):
                value = gath[f, d, sub].astype(F32)
                at = sub * 256 + (d // 2) * 128
                if f == 0 and d % 2 == 1:
                    go[:, at : at + 128] = value
                else:
                    start = at + (0 if f == 0 else 512 + 512 * (d % 2))
                    gq[:, start : start + 128] = value

    part[0, 0] = mm(tok_t, dq[...]).reshape(box).astype(BF16)
    part[0, 1] = mm(att[...], cot[...]).reshape(box).astype(BF16)
    s0 = pair_up(0)
    s0 = spread(0, s0)
    for copy in back:
        copy.wait_recv()
    grad = own[...] + jnp.concatenate([r_o[0], r_o[1]], axis=0).astype(F32)
    mids = []
    zero = jnp.zeros((16, 8, 1024), F32)
    for s in range(sides):
        got = r_s[s].astype(F32)
        mid = got[64:192] + jnp.concatenate([got[0:64], got[192:256]], axis=0)
        mids.append(mid.reshape(16, 8, 1024))
    if sides == 1:
        low = jnp.where(ring == 0, zero, mids[0])
        high = jnp.where(ring == 0, mids[0], zero)
    else:
        low, high = mids
    grad = grad + jnp.concatenate([low, high], axis=1).reshape(256, 1024)
    grad = grad.astype(BF16)
    part[1, 0] = mm(tok_t, grad[:, :512]).reshape(box).astype(BF16)
    part[1, 1] = mm(tok_t, grad[:, 512:]).reshape(box).astype(BF16)
    s1 = pair_up(1)
    s0 = cross(0, s0)
    s1 = spread(1, s1)
    gtok[...] = (
        mm_nt(dq[...], wqkv[:, :512])
        + mm_nt(grad[:, :512], wqkv[:, 512:1024])
        + mm_nt(grad[:, 512:], wqkv[:, 1024:])
    ).astype(BF16)
    s0 = along(0, s0)
    s1 = cross(1, s1)
    s0 = collect(0, s0)
    s1 = along(1, s1)
    finish(0, s0)
    s1 = collect(1, s1)
    finish(1, s1)
    copies.drain()


def vmem(count):
    return [pl.BlockSpec(memory_space=pltpu.VMEM)] * count


def shards(rows, rings, tokens, qkv_weight, out_weight, relative_bias, cotangent):
    sides = 1 if rings == 2 else 2
    share = 512 // (rows * rings)
    tok, cot = tokens.reshape(256, 512), cotangent.reshape(256, 512)
    shape = jax.ShapeDtypeStruct
    sems = pltpu.SemaphoreType.DMA
    count = 2 + 3 * sides
    limit = 48 * 1024 * 1024
    xo, xs = pl.pallas_call(
        functools.partial(halo_kernel, rows, rings, sides),
        out_shape=(shape((512, 512), BF16), shape((sides, 256, 512), BF16)),
        in_specs=vmem(1),
        out_specs=tuple(vmem(2)),
        scratch_shapes=[
            pltpu.VMEM((sides, 128, 512), BF16), sems((count,)), sems((count,)), sems,
        ],
        compiler_params=pltpu.CompilerParams(collective_id=0, has_side_effects=True),
        name="halo",
    )(tok)
    keys = 384 + 192 * sides
    own, oh, sh, dq, att, bias_part = pl.pallas_call(
        functools.partial(attend_kernel, rings, sides),
        out_shape=(
            shape((256, 1024), F32),
            shape((2, 128, 1024), BF16),
            shape((sides, 256, 1024), BF16),
            shape((256, 512), BF16),
            shape((512, 256), BF16),
            shape((8, 17, 17), F32),
        ),
        in_specs=vmem(6),
        out_specs=tuple(vmem(6)),
        scratch_shapes=[
            pltpu.VMEM((512 + 256 * sides, 1024), BF16),
            pltpu.VMEM((256, 512), BF16),
            pltpu.VMEM((256, 512), BF16),
            pltpu.VMEM((192, 128), F32),
            pltpu.VMEM((192 * (16 + 8 * sides), 128), F32),
            pltpu.VMEM((4, keys, 256), F32),
            pltpu.VMEM((4, keys, 256), F32),
        ],
        compiler_params=pltpu.CompilerParams(vmem_limit_bytes=limit),
        name="attend",
    )(xo, xs, cot, qkv_weight, out_weight, relative_bias)
    total_bias = lax.psum(bias_part, ("az", "rng", "dp"))
    count = 2 + 3 * sides + 2 * (1 + 2 * rings + (rows - 1) + 3)

    def buf(*dims):
        return pltpu.VMEM((2,) + dims, BF16)

    gtok, gq, go = pl.pallas_call(
        functools.partial(reduce_kernel, rows, rings, sides, share),
        out_shape=(
            shape((256, 512), BF16), shape((share, 1536), F32), shape((share, 512), F32),
        ),
        in_specs=vmem(8),
        out_specs=tuple(vmem(3)),
        scratch_shapes=[
            buf(128, 1024),
            pltpu.VMEM((sides, 256, 1024), BF16),
            buf(2, rows, rings, share, 512),
            buf(rows, rings, share, 512),
            buf(rows, rings, share, 256),
            buf(2, rows, rings, share, 128),
            buf(rings - 1, rows, share, 256),
            buf(rows, rings, share, 128),
            buf(2, rows, share, 128),
            buf(rows, rings, share, 128),
            buf(rows, share, 128),
            buf(rings - 1, rows, share, 128),
            buf(rows, 2, share, 128),
            buf(rows - 1, 2, share, 128),
            buf(4, 2, share, 128),
            sems((count,)),
            sems((count,)),
        ],
        compiler_params=pltpu.CompilerParams(
            collective_id=1, has_side_effects=True, vmem_limit_bytes=limit
        ),
        name="reduce",
    )(own, oh, sh, dq, att, tok, cot, qkv_weight)
    return gtok.reshape(tokens.shape), gq, go, total_bias


def solution(mesh):
    placed = (P("dp", "az", "rng", None), P(), P(), P(), P("dp", "az", "rng", None))
    return jax.shard_map(
        functools.partial(shards, mesh.shape["az"], mesh.shape["rng"]),
        mesh=mesh,
        in_specs=placed,
        out_specs=(P("dp", "az", "rng", None), P(("az", "rng"), None), P(("az", "rng"), None), P()),
        check_vma=False,
    )
```

time: 398 us -> 125 us (0.31)
  local copies, waits for them, and re-layouts: 157 us -> 9.04 us
  waiting for transfers between devices: 102 us -> 0 us
  Pallas kernels: 0 us -> 74.9 us
  matrix products: 32.3 us -> 0 us
  between operations: 22.3 us -> 0.69 us
  other arithmetic: 20.9 us -> 0 us
  starting transfers between devices: 16.7 us -> 0 us
    psum x1 -> x0, waiting for transfers between devices: 89.1 us -> none  [shards(): lax.psum((local_qkv, local_out, bias_local), ('az', 'rng', 'dp'))]
    pallas_call x0 -> x3, Pallas kernels: none -> 74.9 us  [the longest x1 39.8 us: shards(): pl.pallas_call(functools.partial(reduce_kernel, rows, rings, sides, share...]
    slice x14 -> x0, local copies, waits for them, and re-layouts: 37.9 us -> none  [the longest x4 23.1 us: query_turn(): terms[member]]
    gather x36 -> x0, local copies, waits for them, and re-layouts: 34.5 us -> none
    dot_general x15 -> x0, matrix products: 32.3 us -> none  [the longest x1 4.99 us: bias_grad(): jnp.einsum('hijkl,ikx->hxjl', shaped, along, precision=lax.Precision.HIGH...]
    squeeze x4 -> x0, local copies, waits for them, and re-layouts: 20.1 us -> none  [query_turn(): terms[member]]
    reshape x6 -> x0, local copies, waits for them, and re-layouts: 19.2 us -> none  [the longest x1 13.1 us: query_tile(): lax.dynamic_slice(key_ext, place, (1, ext_side, ext_side, 2 * width))]
    ppermute x8 -> x0, starting transfers between devices: 16.7 us -> none  [the longest x4 9.01 us: extended(): lax.ppermute(tail, axis, [(i, (i + 1) % count) for i in range(ends)])]
  transfers between devices with their start and end apart: 9 -> 0, of which waited for: 4 -> 0; matrix products, arithmetic and copies ran while one was open for 17% -> 0% of each run, Pallas kernels for 0% -> 0%
where the time goes in v1:
time: 125 us
  Pallas kernels  74.9 us (60%)
  blocking collectives  40.1 us (32%)
  local copies, waits for them, and re-layouts  9.04 us (7%)
    psum x1, blocking collectives, shards(): total_bias = lax.psum(bias_part, ('az', 'rng', 'dp'))  40.1 us
    pallas_call x1, Pallas kernels, shards(): pl.pallas_call(functools.partial(reduce_kernel, rows, rings, sides, share...  39.8 us
    pallas_call x1, Pallas kernels, shards(): pl.pallas_call(functools.partial(attend_kernel, rings, sides), out_shape=...  17.8 us
    pallas_call x1, Pallas kernels, shards(): pl.pallas_call(functools.partial(halo_kernel, rows, rings, sides), out_sh...  17.3 us
    unnamed x19, local copies, waits for them, and re-layouts  9.04 us

profile of v1, /device:TPU:0, one launch (start us, length us, event | category | flops | bytes accessed | tf_op | source)
XLA Modules:
  0.0 124.7 jit_solution(6826920798093794235)
XLA Ops:
  0.6 0.9 copy.9.rb
  1.5 17.3 %halo.1 = (bf16[512,512]{1,0:T(8,128)(2,1)}, bf16[1,256,512]{2,1,0:T(8,128)(2,1)}) custom-call(bf16[256,512]{1,0:T(8,128)(2,1)} %bitcast.5), custom_call_target="tpu_custom_call" | custom-call | tf_op jit(solution)/shard_map/halo/pallas_call | solution.py:414
  18.9 0.0 copy-start
  18.9 1.4 %copy-done = bf16[512,1536]{1,0:T(8,128)(2,1)S(1)} copy-done((bf16[512,1536]{1,0:T(8,128)(2,1)S(1)}, bf16[512,1536]{1,0:T(8,128)(2,1)}, u32[]{:S(2)}) %copy-start) | copy-done | bytes 1572888
  20.3 0.0 copy-start.2
  20.3 0.9 copy-done.2
  21.2 0.0 copy-start.4
  21.2 1.0 copy-done.4
  22.3 0.0 copy-start.5
  22.3 1.0 copy-done.5
  23.3 0.0 copy-start.6
  23.3 0.9 copy-done.6
  24.3 0.0 copy-start.1
  24.3 0.0 copy-start.3
  24.3 17.8 %attend.1 = (f32[256,1024]{1,0:T(8,128)S(1)}, bf16[2,128,1024]{2,1,0:T(8,128)(2,1)S(1)}, bf16[1,256,1024]{2,1,0:T(8,128)(2,1)S(1)}, bf16[256,512]{1,0:T(8,128)(2...) custom-call(bf16[512,512]{1,0:T(8,128)(2,1)S(1)} %copy-done.5, bf16[1,256,512]{2,1,0:T(8,128)(2,1)S(1)} %copy-done.6, ...), custom_call_target="tpu_custom_call" | custom-call | tf_op jit(solution)/shard_map/attend/pallas_call | solution.py:426
  42.1 0.0 copy-done.1
  42.1 0.0 copy-done.3
  42.1 39.8 %reduce.1 = (bf16[256,512]{1,0:T(8,128)(2,1)S(1)}, f32[64,1536]{1,0:T(8,128)S(1)}, f32[64,512]{1,0:T(8,128)S(1)}) custom-call(f32[256,1024]{1,0:T(8,128)S(1)} %get-tuple-element.17.own, bf16[2,128,1024]{2,1,0:T(8,128)(2,1)S(1)} %get-tuple-element.18.oh, bf16[1,256,1024]{2,1,0:T(8,128)(2,1)S(1)} %get-tuple-element.19.sh, ...), custom_call_target="tpu_custom_call" | custom-call | tf_op jit(solution)/shard_map/reduce/pallas_call | solution.py:456
  81.9 40.1 %psum.7 = f32[8,17,17]{2,1,0:T(8,128)S(1)} all-reduce(f32[8,17,17]{2,1,0:T(8,128)S(1)} %get-tuple-element.25), channel_id=1, replica_groups=mesh['az'=4,'rng'=2,'dp'=4] {'az','rng','dp'}, use_global_device_ids=true, to_apply=%region_0.0 | all-reduce | flops 2312 | bytes 18496 | tf_op jit(solution)/shard_map/psum | solution.py:450
  122.0 0.6 copy.10
  122.6 0.7 copy.14
  123.3 0.7 copy.15
  124.1 0.7 copy.16
Async XLA Ops:
  18.9 1.4 %copy-start = (bf16[512,1536]{1,0:T(8,128)(2,1)S(1)}, bf16[512,1536]{1,0:T(8,128)(2,1)}, u32[]{:S(2)}) copy-start(bf16[512,1536]{1,0:T(8,128)(2,1)} %wqkv.3) | copy-start | bytes 4718596
  20.3 0.9 copy-start.2
  21.2 1.0 copy-start.4
  22.3 1.0 copy-start.5
  23.3 0.9 copy-start.6
  24.3 17.8 %copy-start.1 = (bf16[512,1536]{1,0:T(8,128)(2,1)S(1)}, bf16[512,1536]{1,0:T(8,128)(2,1)}, u32[]{:S(2)}) copy-start(bf16[512,1536]{1,0:T(8,128)(2,1)} %wqkv.3) | copy-start | bytes 4718596
  24.3 17.8 %copy-start.3 = (bf16[1,16,16,512]{3,2,1,0:T(8,128)(2,1)S(1)}, bf16[1,16,16,512]{3,2,1,0:T(8,128)(2,1)}, u32[]{:S(2)}) copy-start(bf16[1,16,16,512]{3,2,1,0:T(8,128)(2,1)} %param.5) | copy-start | bytes 786436

commit v2 on v1

v2 whole, which is shorter than its diff:
```python
import functools
import math

import jax
import jax.numpy as jnp
from jax import lax
from jax.experimental import pallas as pl
from jax.experimental.pallas import tpu as pltpu
from jax.sharding import PartitionSpec as P

MESH = pl.DeviceIdType.MESH
F32, BF16 = jnp.float32, jnp.bfloat16
NT = (((1,), (1,)), ((), ()))
HIGH = lax.Precision.HIGHEST


def mm(a, b):
    return jnp.dot(a, b, preferred_element_type=F32)


def mm_nt(a, b):
    return lax.dot_general(a, b, NT, preferred_element_type=F32)


class Copies:
    def __init__(self, send, recv):
        self.send, self.recv, self.count, self.made = send, recv, 0, []

    def put(self, src, dst, device):
        copy = pltpu.make_async_remote_copy(
            src_ref=src,
            dst_ref=dst,
            send_sem=self.send.at[self.count],
            recv_sem=self.recv.at[self.count],
            device_id=device,
            device_id_type=MESH,
        )
        copy.start()
        self.count += 1
        self.made.append(copy)
        return copy

    def drain(self):
        for copy in self.made:
            copy.wait_send()


def greet(devices):
    barrier = pltpu.get_barrier_semaphore()
    for device in devices:
        pl.semaphore_signal(barrier, inc=1, device_id=device, device_id_type=MESH)
    pl.semaphore_wait(barrier, len(devices))


def around(rings, rng_at, side):
    return lax.rem(rng_at + (1 if side else rings - 1), rings)


def fused_kernel(
    rows, rings, sides, share,
    tok, wqkv_h, wo_h, rb, cot_h,
    gtok, gq, go, gb_ref,
    xo, xs, edge, wqkv, wo, cot, x_t,
    kv, qs, da, tab, tables, bias, db, dq, att, own, ext, r_o, r_s,
    part, r1, ka, kb, rx, ry, two, ry2, rx2, zin, rz, gath,
    bias_mine, bias_core, bias_y, bias_x, bias_z,
    send, recv, local,
):
    az, ring, dp = lax.axis_index("az"), lax.axis_index("rng"), lax.axis_index("dp")
    up, down = lax.rem(az + rows - 1, rows), lax.rem(az + 1, rows)
    others = [around(rings, ring, side) for side in range(sides)]
    y, core = dp // 2, lax.rem(dp, 2)
    mate, over = y * 2 + 1 - core, (1 - y) * 2 + core
    rng_to = [lax.rem(ring + o, rings) for o in range(1, rings)]
    az_to = [lax.rem(az + o, rows) for o in range(1, rows)]
    dp_to = [lax.rem(dp + o, 4) for o in range(1, 4)]
    loads = [
        pltpu.make_async_copy(tok, xo.at[pl.ds(128, 256)], local.at[0]),
        pltpu.make_async_copy(wqkv_h, wqkv, local.at[1]),
        pltpu.make_async_copy(cot_h, cot, local.at[2]),
        pltpu.make_async_copy(wo_h, wo, local.at[3]),
    ]
    for load in loads:
        load.start()
    greet(
        [(az, other, dp) for other in rng_to]
        + [(at, ring, dp) for at in az_to]
        + [(az, ring, other) for other in dp_to]
        + [(at, other, dp) for other in others for at in (up, down)]
    )
    copies = Copies(send, recv)
    halo = [
        copies.put(tok.at[pl.ds(0, 128)], xo.at[pl.ds(384, 128)], (up, ring, dp)),
        copies.put(tok.at[pl.ds(128, 128)], xo.at[pl.ds(0, 128)], (down, ring, dp)),
    ]
    loads[0].wait()
    cells = xo[128:384, :].astype(F32).reshape(16, 16, 512)
    low_cells = cells[:, :8].reshape(128, 512)
    high_cells = cells[:, 8:].reshape(128, 512)
    for side in range(sides):
        if sides == 1:
            chosen = jnp.where(ring == 0, high_cells, low_cells)
            land = 0
        else:
            chosen = high_cells if side else low_cells
            land = 1 - side
        edge[side] = chosen.astype(BF16)
        src, dst, other = edge.at[side], xs.at[land], others[side]
        halo.append(copies.put(src.at[pl.ds(0, 64)], dst.at[pl.ds(192, 64)], (up, other, dp)))
        halo.append(copies.put(src.at[pl.ds(64, 64)], dst.at[pl.ds(0, 64)], (down, other, dp)))
        halo.append(copies.put(src, dst.at[pl.ds(64, 128)], (az, other, dp)))

    width = 16 + 8 * sides
    lane = lax.broadcasted_iota(jnp.int32, (1, 128), 1)
    group = lane // 16
    inner = lane - group * 16

    tab[...] = jnp.zeros_like(tab)
    for h in range(8):
        tab[h * 24 : h * 24 + 17, 0:17] = rb[h]

    def column(c):
        if c < 16:
            place = jnp.int32(c)
        elif sides == 1:
            place = jnp.where(ring == 0, c, c - 24)
        else:
            place = jnp.int32(c - 24 if c < 24 else c - 8)
        level = ring * 16 + place
        offset = place - inner + 8
        present = (level >= 0) & (level < rings * 16)
        valid = (offset >= 0) & (offset <= 16) & present
        offset = jnp.where(valid, offset, -1)
        hot = lax.broadcasted_iota(jnp.int32, (128, 128), 0) == offset
        return hot.astype(F32), valid

    for c in range(width):
        hot, valid = column(c)
        filled = jnp.dot(tab[...], hot, precision=HIGH, preferred_element_type=F32)
        tables[pl.ds(c, 192, width), :] = jnp.where(valid, filled, -jnp.inf)

    def pieces(a):
        found = [(a * 16, 16, 0)]
        for s in range(sides):
            found.append((384 + 192 * s + a * 8, 8, 16 + 8 * s))
        return found

    def build(p, carry):
        for hh in range(2):
            base = (2 * p + hh) * 24
            for a in range(24):
                block = jnp.full((width, 128), -jnp.inf, F32)
                for q in range(8):
                    i = a - q
                    if 0 <= i <= 16:
                        at = pl.multiple_of((base + i) * width, 8)
                        block = jnp.where(group == q, tables[pl.ds(at, width), :], block)
                for start, size, first in pieces(a):
                    bias[p, start : start + size, hh * 128 : hh * 128 + 128] = block[
                        first : first + size
                    ]
        return carry

    lax.fori_loop(0, 4, build, 0)
    for load in loads[1:]:
        load.wait()
    tokens = xo[128:384, :]
    qs[...] = (mm(tokens, wqkv[:, :512]).astype(BF16).astype(F32) * 0.125).astype(BF16)
    kv[128:384, :] = mm(tokens, wqkv[:, 512:]).astype(BF16)
    da[...] = mm_nt(cot[...], wo[...]).astype(BF16)
    x_t[:, 128:384] = tokens.T
    for copy in halo:
        copy.wait_recv()
    for at in (0, 384):
        cells_at = xo[at : at + 128, :]
        kv[at : at + 128, :] = mm(cells_at, wqkv[:, 512:]).astype(BF16)
        x_t[:, at : at + 128] = cells_at.T
    for s in range(sides):
        at = 512 + 256 * s
        kv[at : at + 256, :] = mm(xs[s], wqkv[:, 512:]).astype(BF16)
        x_t[:, at : at + 256] = xs[s].T

    first_half = lax.broadcasted_iota(jnp.int32, (128, 128), 1) < 64

    def diagonal(block):
        wide = block.astype(F32)
        return jnp.concatenate(
            [jnp.where(first_half, wide, 0.0), jnp.where(first_half, 0.0, wide)], axis=0
        ).astype(BF16)

    def fold(block):
        return jnp.concatenate([block[:64, :128], block[64:, 128:]], axis=0)

    def gather(t, cols):
        parts = [kv[t * 128 : t * 128 + 384, cols]]
        for s in range(sides):
            parts.append(kv[512 + 256 * s + 64 * t : 704 + 256 * s + 64 * t, cols])
        return jnp.concatenate(parts, axis=0)

    def pair(half, p):
        lanes = pl.ds(pl.multiple_of(p * 128, 128), 128)
        v_lanes = pl.ds(pl.multiple_of(512 + p * 128, 128), 128)
        inside = p - 2 * half
        k_ext = pl.ds(pl.multiple_of(inside * 128, 128), 128)
        v_ext = pl.ds(pl.multiple_of(256 + inside * 128, 128), 128)
        grads = []
        for t in range(2):
            cut = slice(t * 128, t * 128 + 128)
            keys, values = gather(t, lanes), gather(t, v_lanes)
            query, d_out = diagonal(qs[cut, lanes]), diagonal(da[cut, lanes])
            score = mm_nt(keys, query) + bias[p]
            e = jnp.exp(score - jnp.max(score, axis=0, keepdims=True))
            prob = e * (1.0 / jnp.sum(e, axis=0, keepdims=True))
            prob_low = prob.astype(BF16)
            attended = fold(mm(values.T, prob_low)).astype(BF16)
            att[lanes, cut] = attended
            terms = da[cut, lanes].astype(F32).T * attended.astype(F32)
            delta = jnp.concatenate(
                [
                    jnp.sum(terms[:64], axis=0, keepdims=True),
                    jnp.sum(terms[64:], axis=0, keepdims=True),
                ],
                axis=1,
            )
            d_score = prob * (mm_nt(values, d_out) - delta)
            if t == 0:
                db[p] = d_score
            else:
                db[p] = db[p] + d_score
            low = d_score.astype(BF16)
            d_query = fold(mm(keys.T, low)) * 0.125
            dq[cut, lanes] = d_query.T.astype(BF16)
            grads.append((mm(low, query), mm(prob_low, d_out)))
        for kind, cols, wide in ((0, k_ext, lanes), (1, v_ext, v_lanes)):
            g0, g1 = grads[0][kind], grads[1][kind]
            mid = g0[128:384] + g1[:256]
            own[:, wide] = mid
            ext[half, 0:128, cols] = g0[:128].astype(BF16)
            ext[half, 128:384, cols] = mid.astype(BF16)
            ext[half, 384:512, cols] = g1[256:384].astype(BF16)
            for s in range(sides):
                b, e0 = 384 + 192 * s, 512 + 256 * s
                ext[half, e0 : e0 + 64, cols] = g0[b : b + 64].astype(BF16)
                ext[half, e0 + 64 : e0 + 192, cols] = (
                    g0[b + 64 : b + 192] + g1[b : b + 128]
                ).astype(BF16)
                ext[half, e0 + 192 : e0 + 256, cols] = g1[b + 128 : b + 192].astype(BF16)

    def send_back(half):
        src = ext.at[half]
        made = [
            copies.put(src.at[pl.ds(0, 128)], r_o.at[half, 1], (up, ring, dp)),
            copies.put(src.at[pl.ds(384, 128)], r_o.at[half, 0], (down, ring, dp)),
        ]
        for s in range(sides):
            e0 = 512 + 256 * s
            dst, other = r_s.at[half, 0 if sides == 1 else 1 - s], others[s]
            made.append(
                copies.put(src.at[pl.ds(e0, 64)], dst.at[pl.ds(192, 64)], (up, other, dp))
            )
            made.append(
                copies.put(src.at[pl.ds(e0 + 192, 64)], dst.at[pl.ds(0, 64)], (down, other, dp))
            )
            made.append(
                copies.put(src.at[pl.ds(e0 + 64, 128)], dst.at[pl.ds(64, 128)], (az, other, dp))
            )
        return made

    x_first = (False, True, False, True)

    def pair_up(u, grad):
        for c in range(2):
            block = grad[:, c * 256 : c * 256 + 256]
            part[u, c] = block.reshape(rows, rings, share, 256).astype(BF16)
        return copies.put(part.at[u, 1 - core], r1.at[u], (az, ring, mate))

    def spread(u, state):
        state.wait_recv()
        kept = part[u, core].astype(F32) + r1[u].astype(F32)
        if x_first[u]:
            ka[u] = kept.astype(BF16)
            return [
                copies.put(ka.at[u, :, to], rx.at[u, o], (az, to, dp))
                for o, to in enumerate(rng_to)
            ]
        kb[u, 0] = kept[..., :128].astype(BF16)
        kb[u, 1] = kept[..., 128:].astype(BF16)
        return [copies.put(kb.at[u, 1 - y], ry.at[u], (az, ring, over))]

    def cross(u, state):
        for copy in state:
            copy.wait_recv()
        if x_first[u]:
            kept = ka[u, :, ring].astype(F32)
            for o in range(rings - 1):
                kept = kept + rx[u, o].astype(F32)
            two[u, 0] = kept[..., :128].astype(BF16)
            two[u, 1] = kept[..., 128:].astype(BF16)
            return [copies.put(two.at[u, 1 - y], ry2.at[u], (az, ring, over))]
        kb[u, y] = (kb[u, y].astype(F32) + ry[u].astype(F32)).astype(BF16)
        return [
            copies.put(kb.at[u, y, :, to], rx2.at[u, o], (az, to, dp))
            for o, to in enumerate(rng_to)
        ]

    def along(u, state):
        for copy in state:
            copy.wait_recv()
        if x_first[u]:
            kept = two[u, y].astype(F32) + ry2[u].astype(F32)
        else:
            kept = kb[u, y, :, ring].astype(F32)
            for o in range(rings - 1):
                kept = kept + rx2[u, o].astype(F32)
        zin[u] = kept.astype(BF16)
        return [
            copies.put(zin.at[u, to], rz.at[u, o], (to, ring, dp)) for o, to in enumerate(az_to)
        ]

    def collect(u, state):
        for copy in state:
            copy.wait_recv()
        kept = zin[u, az].astype(F32)
        for o in range(rows - 1):
            kept = kept + rz[u, o].astype(F32)
        gath[u, dp] = kept.astype(BF16)
        return [copies.put(gath.at[u, dp], gath.at[u, dp], (az, ring, to)) for to in dp_to]

    def finish(u, state):
        for copy in state:
            copy.wait_recv()
        for d in range(4):
            value = gath[u, d].astype(F32)
            at_y, at_c = (d // 2) * 128, d % 2
            if u == 3:
                go[:, at_c * 256 + at_y : at_c * 256 + at_y + 128] = value
            else:
                start = at_c * 256 if u == 2 else 512 + 512 * at_c + 256 * u
                gq[:, start + at_y : start + at_y + 128] = value

    def looped(half):
        def step(p, carry):
            pair(half, p)
            return carry

        lax.fori_loop(2 * half, 2 * half + 2, step, 0)

    looped(0)
    back = send_back(0)
    u0 = pair_up(0, mm(x_t[...], ext[0]))
    looped(1)
    back += send_back(1)
    u0 = spread(0, u0)
    u1 = pair_up(1, mm(x_t[...], ext[1]))
    u2 = pair_up(2, mm(x_t[:, 128:384], dq[...]))
    u3 = pair_up(3, mm(att[...], cot[...]))
    u1 = spread(1, u1)
    u2 = spread(2, u2)
    u3 = spread(3, u3)

    def unbuild(p, carry):
        for hh in range(2):
            base = (2 * p + hh) * 24
            for i in range(17):
                block = jnp.zeros((width, 128), F32)
                for q in range(8):
                    found = [
                        db[p, start : start + size, hh * 128 : hh * 128 + 128]
                        for start, size, _ in pieces(i + q)
                    ]
                    block = jnp.where(group == q, jnp.concatenate(found, axis=0), block)
                tables[pl.ds(pl.multiple_of((base + i) * width, 8), width), :] = block
        return carry

    lax.fori_loop(0, 4, unbuild, 0)
    total = jnp.zeros((192, 128), F32)
    for c in range(width):
        hot, _ = column(c)
        total = total + lax.dot_general(
            tables[pl.ds(c, 192, width), :], hot, NT, precision=HIGH, preferred_element_type=F32
        )
    for h in range(8):
        bias_mine[0, :, h * 32 : h * 32 + 32] = total[h * 24 : h * 24 + 24, 0:32]
    b = copies.put(bias_mine.at[0], bias_core, (az, ring, mate))
    u0 = cross(0, u0)
    u1 = cross(1, u1)
    b.wait_recv()
    bias_mine[1] = bias_mine[0] + bias_core[...]
    b = copies.put(bias_mine.at[1], bias_y, (az, ring, over))
    u2 = cross(2, u2)
    u3 = cross(3, u3)
    b.wait_recv()
    bias_x[ring] = bias_mine[1] + bias_y[...]
    b = [copies.put(bias_x.at[ring], bias_x.at[ring], (az, to, dp)) for to in rng_to]
    u0 = along(0, u0)
    u1 = along(1, u1)
    for copy in b:
        copy.wait_recv()
    bias_z[az] = functools.reduce(jnp.add, [bias_x[r] for r in range(rings)])
    b = [copies.put(bias_z.at[az], bias_z.at[az], (to, ring, dp)) for to in az_to]
    u2 = along(2, u2)
    u3 = along(3, u3)
    u0 = collect(0, u0)
    u1 = collect(1, u1)

    for copy in back:
        copy.wait_recv()
    grads = []
    zero = jnp.zeros((16, 8, 512), F32)
    for half in range(2):
        grad = jnp.concatenate([r_o[half, 0], r_o[half, 1]], axis=0).astype(F32)
        mids = []
        for s in range(sides):
            got = r_s[half, s].astype(F32)
            mid = got[64:192] + jnp.concatenate([got[0:64], got[192:256]], axis=0)
            mids.append(mid.reshape(16, 8, 512))
        if sides == 1:
            low = jnp.where(ring == 0, zero, mids[0])
            high = jnp.where(ring == 0, mids[0], zero)
        else:
            low, high = mids
        grads.append(grad + jnp.concatenate([low, high], axis=1).reshape(256, 512))
    d_key = own[:, :512] + jnp.concatenate([grads[0][:, :256], grads[1][:, :256]], axis=1)
    d_value = own[:, 512:] + jnp.concatenate([grads[0][:, 256:], grads[1][:, 256:]], axis=1)
    gtok[...] = (
        mm_nt(dq[...], wqkv[:, :512])
        + mm_nt(d_key.astype(BF16), wqkv[:, 512:1024])
        + mm_nt(d_value.astype(BF16), wqkv[:, 1024:])
    ).astype(BF16)
    u2 = collect(2, u2)
    u3 = collect(3, u3)
    for copy in b:
        copy.wait_recv()
    summed = functools.reduce(jnp.add, [bias_z[a] for a in range(rows)])
    for h in range(8):
        gb_ref[h] = summed[0:17, h * 32 : h * 32 + 17]
    finish(0, u0)
    finish(1, u1)
    finish(2, u2)
    finish(3, u3)
    copies.drain()


def shards(rows, rings, tokens, qkv_weight, out_weight, relative_bias, cotangent):
    sides = 1 if rings == 2 else 2
    share = 512 // (rows * rings)
    tok, cot = tokens.reshape(256, 512), cotangent.reshape(256, 512)
    shape = jax.ShapeDtypeStruct
    sems = pltpu.SemaphoreType.DMA
    count = 2 + 3 * sides + 2 * (2 + 3 * sides)
    count += 4 * (1 + rings + rows + 2) + 2 + (rings - 1) + (rows - 1)
    keys, cells = 384 + 192 * sides, 512 + 256 * sides

    def low(*dims):
        return pltpu.VMEM(dims, BF16)

    def full(*dims):
        return pltpu.VMEM(dims, F32)

    hbm = pl.BlockSpec(memory_space=pl.ANY)
    vmem = pl.BlockSpec(memory_space=pltpu.VMEM)
    gtok, gq, go, gb = pl.pallas_call(
        functools.partial(fused_kernel, rows, rings, sides, share),
        out_shape=(
            shape((256, 512), BF16),
            shape((share, 1536), F32),
            shape((share, 512), F32),
            shape((8, 17, 17), F32),
        ),
        in_specs=[hbm, hbm, hbm, vmem, hbm],
        out_specs=(vmem, vmem, vmem, vmem),
        scratch_shapes=[
            low(512, 512),
            low(sides, 256, 512),
            low(sides, 128, 512),
            low(512, 1536),
            low(512, 512),
            low(256, 512),
            low(512, cells),
            low(cells, 1024),
            low(256, 512),
            low(256, 512),
            full(192, 128),
            full(192 * (16 + 8 * sides), 128),
            full(4, keys, 256),
            full(4, keys, 256),
            low(256, 512),
            low(512, 256),
            full(256, 1024),
            low(2, cells, 512),
            low(2, 2, 128, 512),
            low(2, sides, 256, 512),
            low(4, 2, rows, rings, share, 256),
            low(4, rows, rings, share, 256),
            low(4, rows, rings, share, 256),
            low(4, 2, rows, rings, share, 128),
            low(4, rings - 1, rows, share, 256),
            low(4, rows, rings, share, 128),
            low(4, 2, rows, share, 128),
            low(4, rows, share, 128),
            low(4, rings - 1, rows, share, 128),
            low(4, rows, share, 128),
            low(4, rows - 1, share, 128),
            low(4, 4, share, 128),
            full(2, 24, 256),
            full(24, 256),
            full(24, 256),
            full(rings, 24, 256),
            full(rows, 24, 256),
            sems((count,)),
            sems((count,)),
            sems((4,)),
        ],
        compiler_params=pltpu.CompilerParams(
            collective_id=0, has_side_effects=True, vmem_limit_bytes=48 * 1024 * 1024
        ),
        name="fused",
    )(tok, qkv_weight, out_weight, relative_bias, cot)
    return gtok.reshape(tokens.shape), gq, go, gb


def solution(mesh):
    placed = (P("dp", "az", "rng", None), P(), P(), P(), P("dp", "az", "rng", None))
    return jax.shard_map(
        functools.partial(shards, mesh.shape["az"], mesh.shape["rng"]),
        mesh=mesh,
        in_specs=placed,
        out_specs=(P("dp", "az", "rng", None), P(("az", "rng"), None), P(("az", "rng"), None), P()),
        check_vma=False,
    )
```

time: 125 us -> 64 us (0.51)
  blocking collectives: 40.1 us -> 0 us
  Pallas kernels: 74.9 us -> 55.1 us
    psum x1 -> x0, blocking collectives: 40.1 us -> none  [shards(): total_bias = lax.psum(bias_part, ('az', 'rng', 'dp'))]
    pallas_call x3 -> x1, Pallas kernels: 74.9 us -> 55.1 us  [shards(): pl.pallas_call(functools.partial(fused_kernel, rows, rings, sides, share)...]
    unnamed x19 -> x13, local copies, waits for them, and re-layouts: 9.04 us -> 7.99 us
where the time goes in v2:
time: 64 us; the launch traced here: 63.7 us
  Pallas kernels  55.1 us (86%)
  local copies, waits for them, and re-layouts  7.99 us (12%)
  between operations  0.66 us (1%)
    pallas_call x1, Pallas kernels, shards(): pl.pallas_call(functools.partial(fused_kernel, rows, rings, sides, share)...  55.1 us
    unnamed x13, local copies, waits for them, and re-layouts  7.99 us

profile of v2, /device:TPU:0, one launch (start us, length us, event | category | flops | bytes accessed | tf_op | source)
XLA Modules:
  0.0 63.7 jit_solution(6595749241880339697)
XLA Ops:
  0.6 0.9 %copy.9.rb = f32[8,17,17]{2,1,0:T(8,128)S(1)} copy(f32[8,17,17]{2,0,1:T(8,128)} %param.8) | data formatting | bytes 18496 | tf_op args[3]
  1.5 0.0 copy-start
  1.5 1.4 %copy-done = bf16[512,1536]{1,0:T(8,128)(2,1)S(1)} copy-done((bf16[512,1536]{1,0:T(8,128)(2,1)S(1)}, bf16[512,1536]{1,0:T(8,128)(2,1)}, u32[]{:S(2)}) %copy-start) | copy-done | bytes 1572888
  2.9 0.0 copy-start.1
  2.9 1.0 %copy-done.1 = bf16[512,512]{1,0:T(8,128)(2,1)S(1)} copy-done((bf16[512,512]{1,0:T(8,128)(2,1)S(1)}, bf16[512,512]{1,0:T(8,128)(2,1)}, u32[]{:S(2)}) %copy-start.1) | copy-done | bytes 524312
  4.0 0.0 copy-start.2
  4.0 0.9 %copy-done.2 = bf16[1,16,16,512]{3,2,1,0:T(8,128)(2,1)S(1)} copy-done((bf16[1,16,16,512]{3,2,1,0:T(8,128)(2,1)S(1)}, bf16[1,16,16,512]{3,2,1,0:T(8,128)(2,1)}, u32[]{:S(2)}) %copy-start.2) | copy-done | bytes 262168
  4.9 0.0 copy-start.3
  4.9 0.9 %copy-done.3 = bf16[1,16,16,512]{3,2,1,0:T(8,128)(2,1)S(1)} copy-done((bf16[1,16,16,512]{3,2,1,0:T(8,128)(2,1)S(1)}, bf16[1,16,16,512]{3,2,1,0:T(8,128)(2,1)}, u32[]{:S(2)}) %copy-start.3) | copy-done | bytes 262168
  5.9 55.1 %fused.1 = (bf16[256,512]{1,0:T(8,128)(2,1)S(1)}, f32[64,1536]{1,0:T(8,128)S(1)}, f32[64,512]{1,0:T(8,128)S(1)}, f32[8,17,17]{2,1,0:T(8,128)S(1)}) custom-call(bf16[256,512]{1,0:T(8,128)(2,1)S(1)} %bitcast.4, bf16[512,1536]{1,0:T(8,128)(2,1)S(1)} %copy-done, bf16[512,512]{1,0:T(8,128)(2,1)S(1)} %copy-done.1, f32[8,17,17]{2,1,0:T(8,128)S(1)} %copy.9.rb, ...), custom_call_target="tpu_custom_call" | custom-call | tf_op jit(solution)/shard_map/fused/pallas_call | solution.py:462
  61.0 0.6 %copy.10 = f32[8,17,17]{2,0,1:T(8,128)} copy(f32[8,17,17]{2,1,0:T(8,128)S(1)} %get-tuple-element.15) | data formatting | bytes 18496
  61.6 0.7 %copy.14 = bf16[1,16,16,512]{3,2,1,0:T(8,128)(2,1)} copy(bf16[1,16,16,512]{3,2,1,0:T(8,128)(2,1)S(1)} %bitcast.3) | data formatting | bytes 524288
  62.3 0.7 %copy.15 = f32[64,1536]{1,0:T(8,128)} copy(f32[64,1536]{1,0:T(8,128)S(1)} %get-tuple-element.21) | data formatting | bytes 786432
  63.1 0.7 %copy.16 = f32[64,512]{1,0:T(8,128)} copy(f32[64,512]{1,0:T(8,128)S(1)} %get-tuple-element.22) | data formatting | bytes 262144
Async XLA Ops:
  1.5 1.4 %copy-start = (bf16[512,1536]{1,0:T(8,128)(2,1)S(1)}, bf16[512,1536]{1,0:T(8,128)(2,1)}, u32[]{:S(2)}) copy-start(bf16[512,1536]{1,0:T(8,128)(2,1)} %wqkv_h.1) | copy-start | bytes 4718596
  2.9 1.0 %copy-start.1 = (bf16[512,512]{1,0:T(8,128)(2,1)S(1)}, bf16[512,512]{1,0:T(8,128)(2,1)}, u32[]{:S(2)}) copy-start(bf16[512,512]{1,0:T(8,128)(2,1)} %wo_h.1) | copy-start | bytes 1572868
  4.0 0.9 %copy-start.2 = (bf16[1,16,16,512]{3,2,1,0:T(8,128)(2,1)S(1)}, bf16[1,16,16,512]{3,2,1,0:T(8,128)(2,1)}, u32[]{:S(2)}) copy-start(bf16[1,16,16,512]{3,2,1,0:T(8,128)(2,1)} %param.5) | copy-start | bytes 786436
  4.9 0.9 %copy-start.3 = (bf16[1,16,16,512]{3,2,1,0:T(8,128)(2,1)S(1)}, bf16[1,16,16,512]{3,2,1,0:T(8,128)(2,1)}, u32[]{:S(2)}) copy-start(bf16[1,16,16,512]{3,2,1,0:T(8,128)(2,1)} %param.9) | copy-start | bytes 786436

commit v3 on v2

--- a/solution.py
+++ b/solution.py
@@ -58,9 +58,9 @@
 
 def fused_kernel(
     rows, rings, sides, share,
-    tok, wqkv_h, wo_h, rb, cot_h,
+    tok, wqkv_h, wo_h, rb_h, cot_h,
     gtok, gq, go, gb_ref,
-    xo, xs, edge, wqkv, wo, cot, x_t,
+    xo, xs, edge, wqkv, wo, cot, rb, x_t,
     kv, qs, da, tab, tables, bias, db, dq, att, own, ext, r_o, r_s,
     part, r1, ka, kb, rx, ry, two, ry2, rx2, zin, rz, gath,
     bias_mine, bias_core, bias_y, bias_x, bias_z,
@@ -79,6 +79,7 @@
         pltpu.make_async_copy(wqkv_h, wqkv, local.at[1]),
         pltpu.make_async_copy(cot_h, cot, local.at[2]),
         pltpu.make_async_copy(wo_h, wo, local.at[3]),
+        pltpu.make_async_copy(rb_h, rb, local.at[4]),
     ]
     for load in loads:
         load.start()
@@ -115,9 +116,9 @@
     group = lane // 16
     inner = lane - group * 16
 
+    loads[4].wait()
     tab[...] = jnp.zeros_like(tab)
-    for h in range(8):
-        tab[h * 24 : h * 24 + 17, 0:17] = rb[h]
+    tab[:, 0:17] = rb[...].reshape(136, 17)
 
     def column(c):
         if c < 16:
@@ -137,7 +138,7 @@
     for c in range(width):
         hot, valid = column(c)
         filled = jnp.dot(tab[...], hot, precision=HIGH, preferred_element_type=F32)
-        tables[pl.ds(c, 192, width), :] = jnp.where(valid, filled, -jnp.inf)
+        tables[pl.ds(c, 136, width), :] = jnp.where(valid, filled, -jnp.inf)
 
     def pieces(a):
         found = [(a * 16, 16, 0)]
@@ -147,13 +148,13 @@
 
     def build(p, carry):
         for hh in range(2):
-            base = (2 * p + hh) * 24
+            head = 2 * p + hh
             for a in range(24):
                 block = jnp.full((width, 128), -jnp.inf, F32)
                 for q in range(8):
                     i = a - q
                     if 0 <= i <= 16:
-                        at = pl.multiple_of((base + i) * width, 8)
+                        at = pl.multiple_of((i * 8 + head) * width, 8)
                         block = jnp.where(group == q, tables[pl.ds(at, width), :], block)
                 for start, size, first in pieces(a):
                     bias[p, start : start + size, hh * 128 : hh * 128 + 128] = block[
@@ -162,7 +163,7 @@
         return carry
 
     lax.fori_loop(0, 4, build, 0)
-    for load in loads[1:]:
+    for load in loads[1:4]:
         load.wait()
     tokens = xo[128:384, :]
     qs[...] = (mm(tokens, wqkv[:, :512]).astype(BF16).astype(F32) * 0.125).astype(BF16)
@@ -203,34 +204,38 @@
         inside = p - 2 * half
         k_ext = pl.ds(pl.multiple_of(inside * 128, 128), 128)
         v_ext = pl.ds(pl.multiple_of(256 + inside * 128, 128), 128)
-        grads = []
-        for t in range(2):
-            cut = slice(t * 128, t * 128 + 128)
-            keys, values = gather(t, lanes), gather(t, v_lanes)
-            query, d_out = diagonal(qs[cut, lanes]), diagonal(da[cut, lanes])
-            score = mm_nt(keys, query) + bias[p]
-            e = jnp.exp(score - jnp.max(score, axis=0, keepdims=True))
-            prob = e * (1.0 / jnp.sum(e, axis=0, keepdims=True))
-            prob_low = prob.astype(BF16)
-            attended = fold(mm(values.T, prob_low)).astype(BF16)
-            att[lanes, cut] = attended
-            terms = da[cut, lanes].astype(F32).T * attended.astype(F32)
-            delta = jnp.concatenate(
+        cuts = [slice(t * 128, t * 128 + 128) for t in range(2)]
+        keys = [gather(t, lanes) for t in range(2)]
+        values = [gather(t, v_lanes) for t in range(2)]
+        query = [diagonal(qs[cut, lanes]) for cut in cuts]
+        d_out = [diagonal(da[cut, lanes]) for cut in cuts]
+        score = [mm_nt(keys[t], query[t]) + bias[p] for t in range(2)]
+        e = [jnp.exp(x - jnp.max(x, axis=0, keepdims=True)) for x in score]
+        d_prob = [mm_nt(values[t], d_out[t]) for t in range(2)]
+        prob = [x * (1.0 / jnp.sum(x, axis=0, keepdims=True)) for x in e]
+        prob_low = [x.astype(BF16) for x in prob]
+        attended = [fold(mm(values[t].T, prob_low[t])).astype(BF16) for t in range(2)]
+        d_value = [mm(prob_low[t], d_out[t]) for t in range(2)]
+        terms = [da[cuts[t], lanes].astype(F32).T * attended[t].astype(F32) for t in range(2)]
+        delta = [
+            jnp.concatenate(
                 [
-                    jnp.sum(terms[:64], axis=0, keepdims=True),
-                    jnp.sum(terms[64:], axis=0, keepdims=True),
+                    jnp.sum(x[:64], axis=0, keepdims=True),
+                    jnp.sum(x[64:], axis=0, keepdims=True),
                 ],
                 axis=1,
             )
-            d_score = prob * (mm_nt(values, d_out) - delta)
-            if t == 0:
-                db[p] = d_score
-            else:
-                db[p] = db[p] + d_score
-            low = d_score.astype(BF16)
-            d_query = fold(mm(keys.T, low)) * 0.125
-            dq[cut, lanes] = d_query.T.astype(BF16)
-            grads.append((mm(low, query), mm(prob_low, d_out)))
+            for x in terms
+        ]
+        d_score = [prob[t] * (d_prob[t] - delta[t]) for t in range(2)]
+        low = [x.astype(BF16) for x in d_score]
+        d_query = [fold(mm(keys[t].T, low[t])) * 0.125 for t in range(2)]
+        d_key = [mm(low[t], query[t]) for t in range(2)]
+        db[p] = d_score[0] + d_score[1]
+        for t in range(2):
+            att[lanes, cuts[t]] = attended[t]
+            dq[cuts[t], lanes] = d_query[t].T.astype(BF16)
+        grads = [(d_key[t], d_value[t]) for t in range(2)]
         for kind, cols, wide in ((0, k_ext, lanes), (1, v_ext, v_lanes)):
             g0, g1 = grads[0][kind], grads[1][kind]
             mid = g0[128:384] + g1[:256]
@@ -266,7 +271,7 @@
             )
         return made
 
-    x_first = (False, True, False, True)
+    x_first = (False, False, False, True)
 
     def pair_up(u, grad):
         for c in range(2):
@@ -360,7 +365,7 @@
 
     def unbuild(p, carry):
         for hh in range(2):
-            base = (2 * p + hh) * 24
+            head = 2 * p + hh
             for i in range(17):
                 block = jnp.zeros((width, 128), F32)
                 for q in range(8):
@@ -369,18 +374,20 @@
                         for start, size, _ in pieces(i + q)
                     ]
                     block = jnp.where(group == q, jnp.concatenate(found, axis=0), block)
-                tables[pl.ds(pl.multiple_of((base + i) * width, 8), width), :] = block
+                tables[pl.ds(pl.multiple_of((i * 8 + head) * width, 8), width), :] = block
         return carry
 
     lax.fori_loop(0, 4, unbuild, 0)
-    total = jnp.zeros((192, 128), F32)
+    total = jnp.zeros((136, 128), F32)
     for c in range(width):
         hot, _ = column(c)
         total = total + lax.dot_general(
-            tables[pl.ds(c, 192, width), :], hot, NT, precision=HIGH, preferred_element_type=F32
+            tables[pl.ds(c, 136, width), :], hot, NT, precision=HIGH, preferred_element_type=F32
         )
-    for h in range(8):
-        bias_mine[0, :, h * 32 : h * 32 + 32] = total[h * 24 : h * 24 + 24, 0:32]
+    for q in range(4):
+        end = min(136, q * 40 + 40)
+        bias_mine[0, 0 : end - q * 40, q * 32 : q * 32 + 32] = total[q * 40 : end, 0:32]
+    bias_mine[0, 16:40, 96:128] = jnp.zeros((24, 32), F32)
     b = copies.put(bias_mine.at[0], bias_core, (az, ring, mate))
     u0 = cross(0, u0)
     u1 = cross(1, u1)
@@ -432,8 +439,10 @@
     for copy in b:
         copy.wait_recv()
     summed = functools.reduce(jnp.add, [bias_z[a] for a in range(rows)])
-    for h in range(8):
-        gb_ref[h] = summed[0:17, h * 32 : h * 32 + 17]
+    for q in range(4):
+        count = min(17, q * 5 + 5) - q * 5
+        piece = summed[0 : count * 8, q * 32 : q * 32 + 17]
+        gb_ref[q * 5 : q * 5 + count] = piece.reshape(count, 8, 17)
     finish(0, u0)
     finish(1, u1)
     finish(2, u2)
@@ -457,7 +466,7 @@
     def full(*dims):
         return pltpu.VMEM(dims, F32)
 
-    hbm = pl.BlockSpec(memory_space=pl.ANY)
+    hbm = pl.BlockSpec(memory_space=pltpu.HBM)
     vmem = pl.BlockSpec(memory_space=pltpu.VMEM)
     gtok, gq, go, gb = pl.pallas_call(
         functools.partial(fused_kernel, rows, rings, sides, share),
@@ -465,9 +474,9 @@
             shape((256, 512), BF16),
             shape((share, 1536), F32),
             shape((share, 512), F32),
-            shape((8, 17, 17), F32),
+            shape((17, 8, 17), F32),
         ),
-        in_specs=[hbm, hbm, hbm, vmem, hbm],
+        in_specs=[hbm] * 5,
         out_specs=(vmem, vmem, vmem, vmem),
         scratch_shapes=[
             low(512, 512),
@@ -476,12 +485,13 @@
             low(512, 1536),
             low(512, 512),
             low(256, 512),
+            full(17, 8, 17),
             low(512, cells),
             low(cells, 1024),
             low(256, 512),
             low(256, 512),
-            full(192, 128),
-            full(192 * (16 + 8 * sides), 128),
+            full(136, 128),
+            full(136 * (16 + 8 * sides), 128),
             full(4, keys, 256),
             full(4, keys, 256),
             low(256, 512),
@@ -502,21 +512,21 @@
             low(4, rows, share, 128),
             low(4, rows - 1, share, 128),
             low(4, 4, share, 128),
-            full(2, 24, 256),
-            full(24, 256),
-            full(24, 256),
-            full(rings, 24, 256),
-            full(rows, 24, 256),
+            full(2, 40, 128),
+            full(40, 128),
+            full(40, 128),
+            full(rings, 40, 128),
+            full(rows, 40, 128),
             sems((count,)),
             sems((count,)),
-            sems((4,)),
+            sems((5,)),
         ],
         compiler_params=pltpu.CompilerParams(
-            collective_id=0, has_side_effects=True, vmem_limit_bytes=48 * 1024 * 1024
+            collective_id=0, has_side_effects=True, vmem_limit_bytes=62 * 1024 * 1024
         ),
         name="fused",
-    )(tok, qkv_weight, out_weight, relative_bias, cot)
-    return gtok.reshape(tokens.shape), gq, go, gb
+    )(tok, qkv_weight, out_weight, relative_bias.transpose(1, 0, 2), cot)
+    return gtok.reshape(tokens.shape), gq, go, gb.transpose(1, 0, 2)
 
 
 def solution(mesh):

time: 64 us -> 58.2 us (0.909)
  Pallas kernels: 55.1 us -> 51.7 us
  local copies, waits for them, and re-layouts: 7.99 us -> 5.67 us
    pallas_call x1, Pallas kernels: 55.1 us -> 51.7 us  [shards(): pl.pallas_call(functools.partial(fused_kernel, rows, rings, sides, share)...]
    unnamed x13 -> x6, local copies, waits for them, and re-layouts: 7.99 us -> 5.67 us
where the time goes in v3:
time: 58.2 us; the launch traced here: 58 us
  Pallas kernels  51.7 us (89%)
  local copies, waits for them, and re-layouts  5.67 us (10%)
  between operations  0.65 us (1%)
    pallas_call x1, Pallas kernels, shards(): pl.pallas_call(functools.partial(fused_kernel, rows, rings, sides, share)...  51.7 us
    unnamed x6, local copies, waits for them, and re-layouts  5.67 us

profile of v3, /device:TPU:0, one launch (start us, length us, event | category | flops | bytes accessed | tf_op | source)
XLA Modules:
  0.0 58.0 jit_solution(2742847880186399549)
XLA Ops:
  0.6 51.7 %fused.1 = (bf16[256,512]{1,0:T(8,128)(2,1)}, f32[64,1536]{1,0:T(8,128)}, f32[64,512]{1,0:T(8,128)}, f32[17,8,17]{2,1,0:T(8,128)}) custom-call(bf16[256,512]{1,0:T(8,128)(2,1)} %bitcast.6, bf16[512,1536]{1,0:T(8,128)(2,1)} %wqkv_h.1, bf16[512,512]{1,0:T(8,128)(2,1)} %wo_h.1, f32[17,8,17]{2,1,0:T(8,128)} %bitcast.9, bf16[256,512]{1,0:T(8,128)(2,1)} %bitcast.7), custom_call_target="tpu_custom_call" | custom-call | tf_op jit(solution)/shard_map/fused/pallas_call | solution.py:471
  52.4 0.0 copy-start
  52.4 1.7 %copy.13 = bf16[1,16,16,512]{3,2,1,0:T(8,128)(2,1)} copy(bf16[1,16,16,512]{3,2,1,0:T(8,128)(2,1)} %bitcast.5) | data formatting | bytes 524288
  54.1 1.8 %copy.14 = f32[64,1536]{1,0:T(8,128)} copy(f32[64,1536]{1,0:T(8,128)} %get-tuple-element.17) | data formatting | bytes 786432
  55.8 1.6 %copy.15 = f32[64,512]{1,0:T(8,128)} copy(f32[64,512]{1,0:T(8,128)} %get-tuple-element.18) | data formatting | bytes 262144
  57.4 0.0 copy-done
  57.4 0.6 %copy.16 = f32[8,17,17]{2,0,1:T(8,128)} copy(f32[8,17,17]{2,0,1:T(8,128)S(1)} %bitcast.8) | data formatting | bytes 18496
Async XLA Ops:
  52.4 5.1 %copy-start = (f32[17,8,17]{2,1,0:T(8,128)S(1)}, f32[17,8,17]{2,1,0:T(8,128)}, u32[]{:S(2)}) copy-start(f32[17,8,17]{2,1,0:T(8,128)} %get-tuple-element.11) | copy-start | bytes 27748

commit v4 on v3

--- a/solution.py
+++ b/solution.py
@@ -60,8 +60,9 @@
     rows, rings, sides, share,
     tok, wqkv_h, wo_h, rb_h, cot_h,
     gtok, gq, go, gb_ref,
-    xo, xs, edge, wqkv, wo, cot, rb, x_t,
-    kv, qs, da, tab, tables, bias, db, dq, att, own, ext, r_o, r_s,
+    xo, xs, edge, co, cs, cot_edge, wqkv, wo, rb, x_t,
+    kv, qs, da, tab, tables, bias, back_bias, db, dq, att, own, ext,
+    stat, stat_edge, stat_az, stat_rng, stat_ext,
     part, r1, ka, kb, rx, ry, two, ry2, rx2, zin, rz, gath,
     bias_mine, bias_core, bias_y, bias_x, bias_z,
     send, recv, local,
@@ -77,7 +78,7 @@
     loads = [
         pltpu.make_async_copy(tok, xo.at[pl.ds(128, 256)], local.at[0]),
         pltpu.make_async_copy(wqkv_h, wqkv, local.at[1]),
-        pltpu.make_async_copy(cot_h, cot, local.at[2]),
+        pltpu.make_async_copy(cot_h, co.at[pl.ds(128, 256)], local.at[2]),
         pltpu.make_async_copy(wo_h, wo, local.at[3]),
         pltpu.make_async_copy(rb_h, rb, local.at[4]),
     ]
@@ -90,26 +91,28 @@
         + [(at, other, dp) for other in others for at in (up, down)]
     )
     copies = Copies(send, recv)
-    halo = [
-        copies.put(tok.at[pl.ds(0, 128)], xo.at[pl.ds(384, 128)], (up, ring, dp)),
-        copies.put(tok.at[pl.ds(128, 128)], xo.at[pl.ds(0, 128)], (down, ring, dp)),
-    ]
-    loads[0].wait()
-    cells = xo[128:384, :].astype(F32).reshape(16, 16, 512)
-    low_cells = cells[:, :8].reshape(128, 512)
-    high_cells = cells[:, 8:].reshape(128, 512)
-    for side in range(sides):
-        if sides == 1:
-            chosen = jnp.where(ring == 0, high_cells, low_cells)
-            land = 0
-        else:
-            chosen = high_cells if side else low_cells
-            land = 1 - side
-        edge[side] = chosen.astype(BF16)
-        src, dst, other = edge.at[side], xs.at[land], others[side]
-        halo.append(copies.put(src.at[pl.ds(0, 64)], dst.at[pl.ds(192, 64)], (up, other, dp)))
-        halo.append(copies.put(src.at[pl.ds(64, 64)], dst.at[pl.ds(0, 64)], (down, other, dp)))
-        halo.append(copies.put(src, dst.at[pl.ds(64, 128)], (az, other, dp)))
+
+    def edges(cells, depth):
+        cells = cells.reshape(16, 16, depth)
+        low, high = cells[:, :8].reshape(128, depth), cells[:, 8:].reshape(128, depth)
+        return [jnp.where(ring == 0, high, low)] if sides == 1 else [low, high]
+
+    def exchange(src, mid, side, edge, ready):
+        made = [
+            copies.put(src.at[pl.ds(0, 128)], mid.at[pl.ds(384, 128)], (up, ring, dp)),
+            copies.put(src.at[pl.ds(128, 128)], mid.at[pl.ds(0, 128)], (down, ring, dp)),
+        ]
+        if ready is not None:
+            ready.wait()
+        for s, chosen in enumerate(edges(mid[128:384, :].astype(F32), 512)):
+            edge[s] = chosen.astype(BF16)
+            near, far, other = edge.at[s], side.at[0 if sides == 1 else 1 - s], others[s]
+            made.append(copies.put(near.at[pl.ds(0, 64)], far.at[pl.ds(192, 64)], (up, other, dp)))
+            made.append(copies.put(near.at[pl.ds(64, 64)], far.at[pl.ds(0, 64)], (down, other, dp)))
+            made.append(copies.put(near, far.at[pl.ds(64, 128)], (az, other, dp)))
+        return made
+
+    halo = exchange(tok, xo, xs, edge, loads[0])
 
     width = 16 + 8 * sides
     lane = lax.broadcasted_iota(jnp.int32, (1, 128), 1)
@@ -120,7 +123,7 @@
     tab[...] = jnp.zeros_like(tab)
     tab[:, 0:17] = rb[...].reshape(136, 17)
 
-    def column(c):
+    def column(c, flipped=False):
         if c < 16:
             place = jnp.int32(c)
         elif sides == 1:
@@ -131,14 +134,15 @@
         offset = place - inner + 8
         present = (level >= 0) & (level < rings * 16)
         valid = (offset >= 0) & (offset <= 16) & present
-        offset = jnp.where(valid, offset, -1)
+        offset = jnp.where(valid, 16 - offset if flipped else offset, -1)
         hot = lax.broadcasted_iota(jnp.int32, (128, 128), 0) == offset
         return hot.astype(F32), valid
 
-    for c in range(width):
-        hot, valid = column(c)
-        filled = jnp.dot(tab[...], hot, precision=HIGH, preferred_element_type=F32)
-        tables[pl.ds(c, 136, width), :] = jnp.where(valid, filled, -jnp.inf)
+    def fill(flipped):
+        for c in range(width):
+            hot, valid = column(c, flipped)
+            filled = jnp.dot(tab[...], hot, precision=HIGH, preferred_element_type=F32)
+            tables[pl.ds(c, 136, width), :] = jnp.where(valid, filled, -jnp.inf)
 
     def pieces(a):
         found = [(a * 16, 16, 0)]
@@ -146,40 +150,64 @@
             found.append((384 + 192 * s + a * 8, 8, 16 + 8 * s))
         return found
 
+    def band(a, head, flipped):
+        block = jnp.full((width, 128), -jnp.inf, F32)
+        for q in range(8):
+            i = a - q
+            if 0 <= i <= 16:
+                row = 16 - i if flipped else i
+                at = pl.multiple_of((row * 8 + head) * width, 8)
+                block = jnp.where(group == q, tables[pl.ds(at, width), :], block)
+        return block
+
     def build(p, carry):
         for hh in range(2):
-            head = 2 * p + hh
             for a in range(24):
-                block = jnp.full((width, 128), -jnp.inf, F32)
-                for q in range(8):
-                    i = a - q
-                    if 0 <= i <= 16:
-                        at = pl.multiple_of((i * 8 + head) * width, 8)
-                        block = jnp.where(group == q, tables[pl.ds(at, width), :], block)
+                block = band(a, 2 * p + hh, False)
                 for start, size, first in pieces(a):
                     bias[p, start : start + size, hh * 128 : hh * 128 + 128] = block[
                         first : first + size
                     ]
         return carry
 
+    def build_back(p, carry):
+        for hh in range(2):
+            cols = slice(hh * 128, hh * 128 + 128)
+            for a in range(24):
+                block = band(a, 2 * p + hh, True)
+                if a < 8:
+                    back_bias[p, a * 16 : a * 16 + 16, cols] = block[:16]
+                elif a >= 16:
+                    back_bias[p, (a - 8) * 16 : (a - 8) * 16 + 16, cols] = block[:16]
+                for s in range(sides):
+                    start = 256 + 192 * s + a * 8
+                    back_bias[p, start : start + 8, cols] = block[16 + 8 * s : 24 + 8 * s]
+        return carry
+
+    fill(True)
+    lax.fori_loop(0, 4, build_back, 0)
+    fill(False)
     lax.fori_loop(0, 4, build, 0)
     for load in loads[1:4]:
         load.wait()
     tokens = xo[128:384, :]
-    qs[...] = (mm(tokens, wqkv[:, :512]).astype(BF16).astype(F32) * 0.125).astype(BF16)
-    kv[128:384, :] = mm(tokens, wqkv[:, 512:]).astype(BF16)
-    da[...] = mm_nt(cot[...], wo[...]).astype(BF16)
-    x_t[:, 128:384] = tokens.T
+
+    def project(cells, at, size):
+        made = mm(cells, wqkv[...]).astype(BF16)
+        qs[at : at + size, :] = (made[:, :512].astype(F32) * 0.125).astype(BF16)
+        kv[at : at + size, :] = made[:, 512:]
+        x_t[:, at : at + size] = cells.T
+
+    project(tokens, 128, 256)
+    da[128:384, :] = mm_nt(co[128:384, :], wo[...]).astype(BF16)
+    stat[...] = jnp.zeros_like(stat)
     for copy in halo:
         copy.wait_recv()
+    cot_halo = exchange(cot_h, co, cs, cot_edge, None)
     for at in (0, 384):
-        cells_at = xo[at : at + 128, :]
-        kv[at : at + 128, :] = mm(cells_at, wqkv[:, 512:]).astype(BF16)
-        x_t[:, at : at + 128] = cells_at.T
+        project(xo[at : at + 128, :], at, 128)
     for s in range(sides):
-        at = 512 + 256 * s
-        kv[at : at + 256, :] = mm(xs[s], wqkv[:, 512:]).astype(BF16)
-        x_t[:, at : at + 256] = xs[s].T
+        project(xs[s], 512 + 256 * s, 256)
 
     first_half = lax.broadcasted_iota(jnp.int32, (128, 128), 1) < 64
 
@@ -205,18 +233,21 @@
         k_ext = pl.ds(pl.multiple_of(inside * 128, 128), 128)
         v_ext = pl.ds(pl.multiple_of(256 + inside * 128, 128), 128)
         cuts = [slice(t * 128, t * 128 + 128) for t in range(2)]
+        ext_cuts = [slice(t * 128 + 128, t * 128 + 256) for t in range(2)]
         keys = [gather(t, lanes) for t in range(2)]
         values = [gather(t, v_lanes) for t in range(2)]
-        query = [diagonal(qs[cut, lanes]) for cut in cuts]
-        d_out = [diagonal(da[cut, lanes]) for cut in cuts]
+        query = [diagonal(qs[cut, lanes]) for cut in ext_cuts]
+        d_out = [diagonal(da[cut, lanes]) for cut in ext_cuts]
         score = [mm_nt(keys[t], query[t]) + bias[p] for t in range(2)]
-        e = [jnp.exp(x - jnp.max(x, axis=0, keepdims=True)) for x in score]
+        top = [jnp.max(x, axis=0, keepdims=True) for x in score]
+        e = [jnp.exp(score[t] - top[t]) for t in range(2)]
+        sums = [jnp.sum(x, axis=0, keepdims=True) for x in e]
         d_prob = [mm_nt(values[t], d_out[t]) for t in range(2)]
-        prob = [x * (1.0 / jnp.sum(x, axis=0, keepdims=True)) for x in e]
+        prob = [e[t] * (1.0 / sums[t]) for t in range(2)]
         prob_low = [x.astype(BF16) for x in prob]
         attended = [fold(mm(values[t].T, prob_low[t])).astype(BF16) for t in range(2)]
         d_value = [mm(prob_low[t], d_out[t]) for t in range(2)]
-        terms = [da[cuts[t], lanes].astype(F32).T * attended[t].astype(F32) for t in range(2)]
+        terms = [da[ext_cuts[t], lanes].astype(F32).T * attended[t].astype(F32) for t in range(2)]
         delta = [
             jnp.concatenate(
                 [
@@ -234,6 +265,11 @@
         db[p] = d_score[0] + d_score[1]
         for t in range(2):
             att[lanes, cuts[t]] = attended[t]
+            lse = top[t] + jnp.log(sums[t])
+            for hh in range(2):
+                side = slice(hh * 128, hh * 128 + 128)
+                stat[t, p, hh : hh + 1, :] = lse[:, side]
+                stat[t, p, 2 + hh : 3 + hh, :] = delta[t][:, side]
             dq[cuts[t], lanes] = d_query[t].T.astype(BF16)
         grads = [(d_key[t], d_value[t]) for t in range(2)]
         for kind, cols, wide in ((0, k_ext, lanes), (1, v_ext, v_lanes)):
@@ -251,25 +287,82 @@
                 ).astype(BF16)
                 ext[half, e0 + 192 : e0 + 256, cols] = g1[b + 128 : b + 192].astype(BF16)
 
-    def send_back(half):
-        src = ext.at[half]
+    def send_stats():
         made = [
-            copies.put(src.at[pl.ds(0, 128)], r_o.at[half, 1], (up, ring, dp)),
-            copies.put(src.at[pl.ds(384, 128)], r_o.at[half, 0], (down, ring, dp)),
+            copies.put(stat.at[0], stat_az.at[1], (up, ring, dp)),
+            copies.put(stat.at[1], stat_az.at[0], (down, ring, dp)),
         ]
+        columns = jnp.concatenate([stat[t].reshape(32, 128).T for t in range(2)], axis=0)
+        for s, chosen in enumerate(edges(columns, 32)):
+            stat_edge[s] = chosen.T
+            near, far, other = stat_edge.at[s], stat_rng.at[0 if sides == 1 else 1 - s], others[s]
+            made.append(copies.put(near, far.at[2], (up, other, dp)))
+            made.append(copies.put(near, far.at[0], (down, other, dp)))
+            made.append(copies.put(near, far.at[1], (az, other, dp)))
+        return made
+
+    def take_stats(made):
+        for copy in made:
+            copy.wait_recv()
+        for t in range(2):
+            stat_ext[t * 128 : t * 128 + 128, 0:32] = stat_az[t].reshape(32, 128).T
         for s in range(sides):
-            e0 = 512 + 256 * s
-            dst, other = r_s.at[half, 0 if sides == 1 else 1 - s], others[s]
-            made.append(
-                copies.put(src.at[pl.ds(e0, 64)], dst.at[pl.ds(192, 64)], (up, other, dp))
+            e0 = 256 + 256 * s
+            stat_ext[e0 : e0 + 64, 0:32] = stat_rng[s, 0].T[64:128]
+            stat_ext[e0 + 64 : e0 + 192, 0:32] = stat_rng[s, 1].T
+            stat_ext[e0 + 192 : e0 + 256, 0:32] = stat_rng[s, 2].T[0:64]
+
+    def take_cotangent():
+        for copy in cot_halo:
+            copy.wait_recv()
+        for at in (0, 384):
+            da[at : at + 128, :] = mm_nt(co[at : at + 128, :], wo[...]).astype(BF16)
+        for s in range(sides):
+            at = 512 + 256 * s
+            da[at : at + 256, :] = mm_nt(cs[s], wo[...]).astype(BF16)
+
+    def back_pair(p):
+        lanes = slice(p * 128, p * 128 + 128)
+        v_lanes = slice(512 + p * 128, 640 + p * 128)
+
+        def cells(ref, t, end, cols):
+            found = [ref[t * end : t * end + 128, cols]]
+            for s in range(sides):
+                at = end + 128 + 256 * s + 64 * t
+                found.append(ref[at : at + 192, cols])
+            return jnp.concatenate(found, axis=0)
+
+        def bands(t):
+            found = [back_bias[p, t * 128 : t * 128 + 128, :]]
+            for s in range(sides):
+                found.append(back_bias[p, 256 + 192 * s : 448 + 192 * s, :])
+            return jnp.concatenate(found, axis=0)
+
+        def both(stats, k):
+            return jnp.concatenate(
+                [jnp.broadcast_to(stats[:, k + h : k + h + 1], (stats.shape[0], 128)) for h in (0, 1)],
+                axis=1,
             )
-            made.append(
-                copies.put(src.at[pl.ds(e0 + 192, 64)], dst.at[pl.ds(0, 64)], (down, other, dp))
-            )
-            made.append(
-                copies.put(src.at[pl.ds(e0 + 64, 128)], dst.at[pl.ds(64, 128)], (az, other, dp))
-            )
-        return made
+
+        tiles = range(2)
+        query = [cells(qs, t, 384, lanes) for t in tiles]
+        d_out = [cells(da, t, 384, lanes) for t in tiles]
+        stats = [cells(stat_ext, t, 128, slice(0, 32)) for t in tiles]
+        mine = [slice(t * 128 + 128, t * 128 + 256) for t in tiles]
+        keys = [diagonal(kv[cut, lanes]) for cut in mine]
+        values = [diagonal(kv[cut, v_lanes]) for cut in mine]
+        score = [mm_nt(query[t], keys[t]) + bands(t) for t in tiles]
+        d_prob = [mm_nt(d_out[t], values[t]) for t in tiles]
+        prob = [jnp.exp(score[t] - both(stats[t], p * 8)) for t in tiles]
+        low = [
+            (prob[t] * (d_prob[t] - both(stats[t], p * 8 + 2))).astype(BF16) for t in tiles
+        ]
+        d_key = [fold(mm(query[t].T, low[t])) for t in tiles]
+        d_value = [fold(mm(d_out[t].T, prob[t].astype(BF16))) for t in tiles]
+        for t in tiles:
+            rows_at = slice(t * 128, t * 128 + 128)
+            own[rows_at, lanes] = own[rows_at, lanes] + d_key[t].T
+            own[rows_at, v_lanes] = own[rows_at, v_lanes] + d_value[t].T
 
     x_first = (False, False, False, True)
 
@@ -351,14 +444,13 @@
         lax.fori_loop(2 * half, 2 * half + 2, step, 0)
 
     looped(0)
-    back = send_back(0)
     u0 = pair_up(0, mm(x_t[...], ext[0]))
     looped(1)
-    back += send_back(1)
+    stats_out = send_stats()
     u0 = spread(0, u0)
     u1 = pair_up(1, mm(x_t[...], ext[1]))
     u2 = pair_up(2, mm(x_t[:, 128:384], dq[...]))
-    u3 = pair_up(3, mm(att[...], cot[...]))
+    u3 = pair_up(3, mm(att[...], co[128:384, :]))
     u1 = spread(1, u1)
     u2 = spread(2, u2)
     u3 = spread(3, u3)
@@ -390,52 +482,38 @@
     bias_mine[0, 16:40, 96:128] = jnp.zeros((24, 32), F32)
     b = copies.put(bias_mine.at[0], bias_core, (az, ring, mate))
     u0 = cross(0, u0)
-    u1 = cross(1, u1)
+    take_cotangent()
+    take_stats(stats_out)
+    back_pair(0)
     b.wait_recv()
     bias_mine[1] = bias_mine[0] + bias_core[...]
     b = copies.put(bias_mine.at[1], bias_y, (az, ring, over))
-    u2 = cross(2, u2)
+    u1 = cross(1, u1)
     u3 = cross(3, u3)
+    u0 = along(0, u0)
+    back_pair(1)
     b.wait_recv()
     bias_x[ring] = bias_mine[1] + bias_y[...]
     b = [copies.put(bias_x.at[ring], bias_x.at[ring], (az, to, dp)) for to in rng_to]
-    u0 = along(0, u0)
+    u2 = cross(2, u2)
     u1 = along(1, u1)
+    back_pair(2)
     for copy in b:
         copy.wait_recv()
     bias_z[az] = functools.reduce(jnp.add, [bias_x[r] for r in range(rings)])
     b = [copies.put(bias_z.at[az], bias_z.at[az], (to, ring, dp)) for to in az_to]
+    u3 = along(3, u3)
     u2 = along(2, u2)
-    u3 = along(3, u3)
     u0 = collect(0, u0)
     u1 = collect(1, u1)
-
-    for copy in back:
-        copy.wait_recv()
-    grads = []
-    zero = jnp.zeros((16, 8, 512), F32)
-    for half in range(2):
-        grad = jnp.concatenate([r_o[half, 0], r_o[half, 1]], axis=0).astype(F32)
-        mids = []
-        for s in range(sides):
-            got = r_s[half, s].astype(F32)
-            mid = got[64:192] + jnp.concatenate([got[0:64], got[192:256]], axis=0)
-            mids.append(mid.reshape(16, 8, 512))
-        if sides == 1:
-            low = jnp.where(ring == 0, zero, mids[0])
-            high = jnp.where(ring == 0, mids[0], zero)
-        else:
-            low, high = mids
-        grads.append(grad + jnp.concatenate([low, high], axis=1).reshape(256, 512))
-    d_key = own[:, :512] + jnp.concatenate([grads[0][:, :256], grads[1][:, :256]], axis=1)
-    d_value = own[:, 512:] + jnp.concatenate([grads[0][:, 256:], grads[1][:, 256:]], axis=1)
+    back_pair(3)
+    u3 = collect(3, u3)
+    u2 = collect(2, u2)
     gtok[...] = (
         mm_nt(dq[...], wqkv[:, :512])
-        + mm_nt(d_key.astype(BF16), wqkv[:, 512:1024])
-        + mm_nt(d_value.astype(BF16), wqkv[:, 1024:])
+        + mm_nt(own[:, :512].astype(BF16), wqkv[:, 512:1024])
+        + mm_nt(own[:, 512:].astype(BF16), wqkv[:, 1024:])
     ).astype(BF16)
-    u2 = collect(2, u2)
-    u3 = collect(3, u3)
     for copy in b:
         copy.wait_recv()
     summed = functools.reduce(jnp.add, [bias_z[a] for a in range(rows)])
@@ -450,6 +528,15 @@
     copies.drain()
 
 
+def leave_kernel(*refs):
+    sem = refs[8]
+    moves = [pltpu.make_async_copy(refs[i], refs[4 + i], sem.at[i]) for i in range(4)]
+    for move in moves:
+        move.start()
+    for move in moves:
+        move.wait()
+
+
 def shards(rows, rings, tokens, qkv_weight, out_weight, relative_bias, cotangent):
     sides = 1 if rings == 2 else 2
     share = 512 // (rows * rings)
@@ -468,7 +555,7 @@
 
     hbm = pl.BlockSpec(memory_space=pltpu.HBM)
     vmem = pl.BlockSpec(memory_space=pltpu.VMEM)
-    gtok, gq, go, gb = pl.pallas_call(
+    made = pl.pallas_call(
         functools.partial(fused_kernel, rows, rings, sides, share),
         out_shape=(
             shape((256, 512), BF16),
@@ -482,24 +569,30 @@
             low(512, 512),
             low(sides, 256, 512),
             low(sides, 128, 512),
+            low(512, 512),
+            low(sides, 256, 512),
+            low(sides, 128, 512),
             low(512, 1536),
             low(512, 512),
-            low(256, 512),
             full(17, 8, 17),
             low(512, cells),
             low(cells, 1024),
-            low(256, 512),
-            low(256, 512),
+            low(cells, 512),
+            low(cells, 512),
             full(136, 128),
             full(136 * (16 + 8 * sides), 128),
             full(4, keys, 256),
+            full(4, keys - 128, 256),
             full(4, keys, 256),
             low(256, 512),
             low(512, 256),
             full(256, 1024),
             low(2, cells, 512),
-            low(2, 2, 128, 512),
-            low(2, sides, 256, 512),
+            full(2, 4, 8, 128),
+            full(sides, 32, 128),
+            full(2, 4, 8, 128),
+            full(sides, 3, 32, 128),
+            full(256 + 256 * sides, 128),
             low(4, 2, rows, rings, share, 256),
             low(4, rows, rings, share, 256),
             low(4, rows, rings, share, 256),
@@ -526,6 +619,15 @@
         ),
         name="fused",
     )(tok, qkv_weight, out_weight, relative_bias.transpose(1, 0, 2), cot)
+    gtok, gq, go, gb = pl.pallas_call(
+        leave_kernel,
+        out_shape=tuple(shape(x.shape, x.dtype) for x in made),
+        in_specs=[hbm] * 4,
+        out_specs=(hbm,) * 4,
+        scratch_shapes=[sems((4,))],
+        compiler_params=pltpu.CompilerParams(vmem_limit_bytes=62 * 1024 * 1024),
+        name="leave",
+    )(*made)
     return gtok.reshape(tokens.shape), gq, go, gb.transpose(1, 0, 2)
 
 

time: 58.2 us -> 80.7 us (1.39)
  Pallas kernels: 51.7 us -> 79.7 us
  local copies, waits for them, and re-layouts: 5.67 us -> 0 us
    pallas_call x0 -> x1, Pallas kernels: none -> 27.1 us  [shards(): pl.pallas_call(leave_kernel, out_shape=tuple((shape(x.shape, x.dtype) for...]
    unnamed x6 -> x0, local copies, waits for them, and re-layouts: 5.67 us -> none
    pallas_call x1, Pallas kernels: 51.7 us -> 52.6 us  [shards(): pl.pallas_call(functools.partial(fused_kernel, rows, rings, sides, share)...]
where the time goes in v4:
time: 80.7 us; the launch traced here: 80.5 us
  Pallas kernels  79.7 us (99%)
  between operations  0.82 us (1%)
    pallas_call x1, Pallas kernels, shards(): pl.pallas_call(functools.partial(fused_kernel, rows, rings, sides, share)...  52.6 us
    pallas_call x1, Pallas kernels, shards(): pl.pallas_call(leave_kernel, out_shape=tuple((shape(x.shape, x.dtype) for...  27.1 us

profile of v4, /device:TPU:0, one launch (start us, length us, event | category | flops | bytes accessed | tf_op | source)
XLA Modules:
  0.0 80.5 jit_solution(17258756569720769824)
XLA Ops:
  0.6 52.6 %fused.1 = (bf16[256,512]{1,0:T(8,128)(2,1)}, f32[64,1536]{1,0:T(8,128)}, f32[64,512]{1,0:T(8,128)}, f32[17,8,17]{2,1,0:T(8,128)}) custom-call(bf16[256,512]{1,0:T(8,128)(2,1)} %bitcast.5, bf16[512,1536]{1,0:T(8,128)(2,1)} %wqkv_h.1, bf16[512,512]{1,0:T(8,128)(2,1)} %wo_h.1, f32[17,8,17]{2,1,0:T(8,128)} %bitcast.7, bf16[256,512]{1,0:T(8,128)(2,1)} %bitcast.6), custom_call_target="tpu_custom_call" | custom-call | tf_op jit(solution)/shard_map/fused/pallas_call | solution.py:558
  53.3 27.1 %leave.1 = (bf16[256,512]{1,0:T(8,128)(2,1)}, f32[64,1536]{1,0:T(8,128)}, f32[64,512]{1,0:T(8,128)}, f32[17,8,17]{2,1,0:T(8,128)}) custom-call(bf16[256,512]{1,0:T(8,128)(2,1)} %get-tuple-element.12.refs_0_, f32[64,1536]{1,0:T(8,128)} %get-tuple-element.13.refs_1_, f32[64,512]{1,0:T(8,128)} %get-tuple-element.14.refs_2_, f32[17,8,17]{2,1,0:T(8,128)} %get-tuple-element.15.refs_3_), custom_call_target="tpu_custom_call" | custom-call | tf_op jit(solution)/shard_map/leave/pallas_call | solution.py:622

commit v5 on v3

--- a/solution.py
+++ b/solution.py
@@ -11,7 +11,6 @@
 MESH = pl.DeviceIdType.MESH
 F32, BF16 = jnp.float32, jnp.bfloat16
 NT = (((1,), (1,)), ((), ()))
-HIGH = lax.Precision.HIGHEST
 
 
 def mm(a, b):
@@ -133,11 +132,20 @@
         valid = (offset >= 0) & (offset <= 16) & present
         offset = jnp.where(valid, offset, -1)
         hot = lax.broadcasted_iota(jnp.int32, (128, 128), 0) == offset
-        return hot.astype(F32), valid
-
+        return hot.astype(BF16), valid
+
+    def split(block, count):
+        found = []
+        for _ in range(count):
+            found.append(block.astype(BF16))
+            block = block - found[-1].astype(F32)
+        return jnp.concatenate(found, axis=0)
+
+    tab_parts = split(tab[...], 3)
     for c in range(width):
         hot, valid = column(c)
-        filled = jnp.dot(tab[...], hot, precision=HIGH, preferred_element_type=F32)
+        filled = mm(tab_parts, hot)
+        filled = filled[:136] + filled[136:272] + filled[272:]
         tables[pl.ds(c, 136, width), :] = jnp.where(valid, filled, -jnp.inf)
 
     def pieces(a):
@@ -381,9 +389,8 @@
     total = jnp.zeros((136, 128), F32)
     for c in range(width):
         hot, _ = column(c)
-        total = total + lax.dot_general(
-            tables[pl.ds(c, 136, width), :], hot, NT, precision=HIGH, preferred_element_type=F32
-        )
+        folded = mm_nt(split(tables[pl.ds(c, 136, width), :], 2), hot)
+        total = total + folded[:136] + folded[136:]
     for q in range(4):
         end = min(136, q * 40 + 40)
         bias_mine[0, 0 : end - q * 40, q * 32 : q * 32 + 32] = total[q * 40 : end, 0:32]
@@ -440,14 +447,29 @@
         copy.wait_recv()
     summed = functools.reduce(jnp.add, [bias_z[a] for a in range(rows)])
     for q in range(4):
-        count = min(17, q * 5 + 5) - q * 5
-        piece = summed[0 : count * 8, q * 32 : q * 32 + 17]
-        gb_ref[q * 5 : q * 5 + count] = piece.reshape(count, 8, 17)
+        end = min(136, q * 40 + 40)
+        gb_ref[q * 40 : end, 0:32] = summed[0 : end - q * 40, q * 32 : q * 32 + 32]
     finish(0, u0)
     finish(1, u1)
     finish(2, u2)
     finish(3, u3)
     copies.drain()
+
+
+def leave_kernel(*refs):
+    source, target, held, sem = refs[:4], refs[4:8], refs[8:12], refs[12]
+    loads = [pltpu.make_async_copy(source[i], held[i], sem.at[i]) for i in range(4)]
+    for load in loads:
+        load.start()
+    stores = []
+    for i in range(3):
+        loads[i].wait()
+        stores.append(pltpu.make_async_copy(held[i], target[i], sem.at[4 + i]))
+        stores[-1].start()
+    loads[3].wait()
+    target[3][...] = held[3][:, 0:17].reshape(17, 8, 17)
+    for store in stores:
+        store.wait()
 
 
 def shards(rows, rings, tokens, qkv_weight, out_weight, relative_bias, cotangent):
@@ -468,13 +490,13 @@
 
     hbm = pl.BlockSpec(memory_space=pltpu.HBM)
     vmem = pl.BlockSpec(memory_space=pltpu.VMEM)
-    gtok, gq, go, gb = pl.pallas_call(
+    made = pl.pallas_call(
         functools.partial(fused_kernel, rows, rings, sides, share),
         out_shape=(
             shape((256, 512), BF16),
             shape((share, 1536), F32),
             shape((share, 512), F32),
-            shape((17, 8, 17), F32),
+            shape((136, 128), F32),
         ),
         in_specs=[hbm] * 5,
         out_specs=(vmem, vmem, vmem, vmem),
@@ -526,6 +548,15 @@
         ),
         name="fused",
     )(tok, qkv_weight, out_weight, relative_bias.transpose(1, 0, 2), cot)
+    gtok, gq, go, gb = pl.pallas_call(
+        leave_kernel,
+        out_shape=tuple(shape(x.shape, x.dtype) for x in made[:3]) + (shape((17, 8, 17), F32),),
+        in_specs=[hbm] * 4,
+        out_specs=(hbm, hbm, hbm, vmem),
+        scratch_shapes=[pltpu.VMEM(x.shape, x.dtype) for x in made] + [sems((8,))],
+        compiler_params=pltpu.CompilerParams(vmem_limit_bytes=62 * 1024 * 1024),
+        name="leave",
+    )(*made)
     return gtok.reshape(tokens.shape), gq, go, gb.transpose(1, 0, 2)
 
 

time: 58.2 us -> 55.1 us (0.947)
  local copies, waits for them, and re-layouts: 5.67 us -> 0 us
  Pallas kernels: 51.7 us -> 54.3 us
    unnamed x6 -> x0, local copies, waits for them, and re-layouts: 5.67 us -> none
    pallas_call x0 -> x1, Pallas kernels: none -> 2.56 us  [shards(): pl.pallas_call(leave_kernel, out_shape=tuple((shape(x.shape, x.dtype) for...]
where the time goes in v5:
time: 55.1 us; the launch traced here: 55 us
  Pallas kernels  54.3 us (99%)
  between operations  0.64 us (1%)
    pallas_call x1, Pallas kernels, shards(): pl.pallas_call(functools.partial(fused_kernel, rows, rings, sides, share)...  51.8 us
    pallas_call x1, Pallas kernels, shards(): pl.pallas_call(leave_kernel, out_shape=tuple((shape(x.shape, x.dtype) for...  2.56 us

profile of v5, /device:TPU:0, one launch (start us, length us, event | category | flops | bytes accessed | tf_op | source)
XLA Modules:
  0.0 55.0 jit_solution(177355459094471548)
XLA Ops:
  0.6 51.8 %fused.1 = (bf16[256,512]{1,0:T(8,128)(2,1)}, f32[64,1536]{1,0:T(8,128)}, f32[64,512]{1,0:T(8,128)}, f32[136,128]{1,0:T(8,128)}) custom-call(bf16[256,512]{1,0:T(8,128)(2,1)} %bitcast.5, bf16[512,1536]{1,0:T(8,128)(2,1)} %wqkv_h.1, bf16[512,512]{1,0:T(8,128)(2,1)} %wo_h.1, f32[17,8,17]{2,1,0:T(8,128)} %bitcast.7, bf16[256,512]{1,0:T(8,128)(2,1)} %bitcast.6), custom_call_target="tpu_custom_call" | custom-call | tf_op jit(solution)/shard_map/fused/pallas_call | solution.py:493
  52.4 2.6 %leave.1 = (bf16[256,512]{1,0:T(8,128)(2,1)}, f32[64,1536]{1,0:T(8,128)}, f32[64,512]{1,0:T(8,128)}, f32[17,8,17]{2,1,0:T(8,128)}) custom-call(bf16[256,512]{1,0:T(8,128)(2,1)} %get-tuple-element.12.refs_0_, f32[64,1536]{1,0:T(8,128)} %get-tuple-element.13.refs_1_, f32[64,512]{1,0:T(8,128)} %get-tuple-element.14.refs_2_, f32[136,128]{1,0:T(8,128)} %get-tuple-element.15.refs_3_), custom_call_target="tpu_custom_call" | custom-call | tf_op jit(solution)/shard_map/leave/pallas_call | solution.py:551
